TPU v7x, 128 devices: a whole 4x4x4 slice. The times are simulated.
128 devices in a mesh: row: 16 (over x, z), col: 8 (over y, core).
Axes of the slice: x: 4, y: 4, z: 4, core: 2. Of those that a mesh axis runs over, the one named last changes fastest.
Arguments:
- loader_rows: bfloat16 [256, 32, 6144], P('row', None, 'col'), may hold values from -6 to 6
- packing: int32 [256], P('row'), may hold values from 0 to 255, as said below
- segment_ids: int32 [16, 512], P('row'), may hold values from 0 to 5, never falling along the last dimension, each value on 1 to 160 neighbouring positions
- qkv_weight: bfloat16 [6144, 9216], P('row', 'col'), may hold values from -0.078125 to 0.078125
- gain_query: float32 [24, 128], P('col'), may hold values from 0.1 to 1.9
- gain_key: float32 [24, 128], P('col'), may hold values from 0.1 to 1.9
- out_grad: bfloat16 [8192, 3072], P('row', 'col'), may hold values from -6 to 6
Outputs:
- attn_out: bfloat16 [8192, 3072], P('row', 'col')
- grad_rows: bfloat16 [8192, 6144], P('row', 'col')
- grad_weight: bfloat16 [6144, 9216], P('row', 'col')
Inputs may be any that keep to these rules, and one draw needn't show every extreme that they name: packing is a permutation of the 256 block slots. Block slots o * 16 to o * 16 + 15 belong to owner o; the 16 blocks of one loader device (aligned runs of 16 entries) send at most 2 blocks to one owner, and exactly 2 to some owner in every draw.
All inputs are finite; a program needn't handle non-finite values.
Results may differ from a plain program's by a relative error of at most 0.02.
Values may be sent and summed in bfloat16 or wider, within the bound.
No kernel may reach another device: no remote copies, remote signals or barrier semaphores. Data moves between devices by JAX's collectives and lax.ppermute only.
A program may use at most 192 MiB of HBM per device.

v0:
```python
import jax
import jax.numpy as jnp
from jax import lax
from jax.experimental import pallas as pl
from jax.experimental.pallas import tpu as pltpu
from jax.sharding import PartitionSpec as P

CAP = 2
N_RING = 4
LABEL_COLS = 128
VMEM_BYTES = 56 * 1024 * 1024


def along_col(dy, dc):
    return [
        (y * 2 + c, ((y + dy) % N_RING) * 2 + (c + dc) % 2) for y in range(N_RING) for c in range(2)
    ]


def along_row(dx, dz):
    return [
        (x * N_RING + z, ((x + dx) % N_RING) * N_RING + (z + dz) % N_RING)
        for x in range(N_RING)
        for z in range(N_RING)
    ]


def send_x(values, step):
    return lax.ppermute(values, "row", along_row(step, 0))


def send_z(values, step):
    return lax.ppermute(values, "row", along_row(0, step))


def send_y(values, step):
    return lax.ppermute(values, "col", along_col(step, 0))


def send_to_half(values, step):
    pairs = []
    for place in range(N_RING * N_RING):
        x, z = divmod(place, N_RING)
        to = (z + step) % N_RING
        for y in range(N_RING):
            col = 2 * y + to // 2
            pairs.append((place * 2 * N_RING + col, (x * N_RING + to) * 2 * N_RING + col))
    return lax.ppermute(values, ("row", "col"), pairs)


def swap_core(values):
    return lax.ppermute(values, "col", along_col(0, 1))


def pack_kernel(packing, blocks, outgoing, source, label, count):
    owners = outgoing.shape[0]
    block_count, block_rows, cols = blocks.shape
    label_rows = block_rows // CAP
    for owner in range(owners):
        count[owner] = 0
    for slot in range(owners * CAP):
        source[slot] = 0
        label[slot] = -1

    def route(block, carry):
        target = packing[block]
        owner = target // block_count
        rank = count[owner]
        count[owner] = rank + 1
        source[owner * CAP + rank] = block
        label[owner * CAP + rank] = target - owner * block_count
        return carry

    lax.fori_loop(0, block_count, route, 0)

    def fill(owner, carry):
        for rank in range(CAP):
            slot = owner * CAP + rank
            outgoing[owner, :, rank * cols : (rank + 1) * cols] = blocks[source[slot]]
            mark = jnp.full((label_rows, LABEL_COLS), label[slot], jnp.int32).astype(jnp.float32)
            outgoing[owner, rank * label_rows : (rank + 1) * label_rows, CAP * cols :] = mark.astype(
                jnp.bfloat16
            )
        return carry

    lax.fori_loop(0, owners, fill, 0)


def pack_blocks(packing, blocks, owners):
    block_count, block_rows, cols = blocks.shape
    return pl.pallas_call(
        pack_kernel,
        out_shape=jax.ShapeDtypeStruct((owners, block_rows, CAP * cols + LABEL_COLS), blocks.dtype),
        in_specs=[
            pl.BlockSpec(memory_space=pltpu.SMEM),
            pl.BlockSpec(memory_space=pltpu.VMEM),
        ],
        out_specs=pl.BlockSpec(memory_space=pltpu.VMEM),
        scratch_shapes=[
            pltpu.SMEM((owners * CAP,), jnp.int32),
            pltpu.SMEM((owners * CAP,), jnp.int32),
            pltpu.SMEM((owners,), jnp.int32),
        ],
        compiler_params=pltpu.CompilerParams(vmem_limit_bytes=VMEM_BYTES),
    )(packing, blocks)


def place_kernel(where, arrived, rows):
    cols = rows.shape[2]

    def place(slot, carry):
        spot = where[slot]
        start = pl.multiple_of((spot % CAP) * cols, cols)
        rows[slot] = arrived[spot // CAP, :, pl.ds(start, cols)]
        return carry

    lax.fori_loop(0, rows.shape[0], place, 0)


def place_blocks(arrived, block_count):
    owners, block_rows, cols = arrived.shape
    cols = (cols - LABEL_COLS) // CAP
    label = arrived[:, :: block_rows // CAP, CAP * cols]
    label = label.astype(jnp.int32).reshape(owners * CAP)
    spots = jnp.arange(owners * CAP, dtype=jnp.int32)
    hit = jnp.arange(block_count, dtype=jnp.int32)[:, None] == label[None, :]
    where = jnp.sum(jnp.where(hit, spots[None, :], 0), axis=1)
    return pl.pallas_call(
        place_kernel,
        out_shape=jax.ShapeDtypeStruct((block_count, block_rows, cols), arrived.dtype),
        in_specs=[
            pl.BlockSpec(memory_space=pltpu.SMEM),
            pl.BlockSpec(memory_space=pltpu.VMEM),
        ],
        out_specs=pl.BlockSpec(memory_space=pltpu.VMEM),
        compiler_params=pltpu.CompilerParams(vmem_limit_bytes=VMEM_BYTES),
    )(where, arrived)


def dot(left, right, left_dim, right_dim):
    return lax.dot_general(
        left, right, (((left_dim,), (right_dim,)), ((), ())), preferred_element_type=jnp.float32
    )


def normalize(values):
    centred = values - jnp.mean(values, axis=-1, keepdims=True)
    inv_std = lax.rsqrt(jnp.mean(centred * centred, axis=-1, keepdims=True) + 1e-06)
    return (centred * inv_std, inv_std)


def norm_grad(upstream, normed, inv_std, gain):
    scaled = upstream * gain
    mean_one = jnp.mean(scaled, axis=-1, keepdims=True)
    mean_two = jnp.mean(scaled * normed, axis=-1, keepdims=True)
    return (scaled - mean_one - normed * mean_two) * inv_std


def attend(projected, gain_query, gain_key, seg_col, seg_row, up):
    size = up.shape[1]
    query_hat, query_inv = normalize(projected[:, :size])
    key_hat, key_inv = normalize(projected[:, size : 2 * size])
    query = (query_hat * gain_query).astype(jnp.bfloat16)
    key = (key_hat * gain_key).astype(jnp.bfloat16)
    value = projected[:, 2 * size :].astype(jnp.bfloat16)
    factor = 1.0 / size**0.5
    weights = jnp.exp(dot(query, key, 1, 1) * factor)
    weights = jnp.where(seg_col == seg_row, weights, 0.0)
    probs = weights * (1.0 / jnp.sum(weights, axis=-1, keepdims=True))
    probs_half = probs.astype(jnp.bfloat16)
    out = dot(probs_half, value, 1, 0).astype(jnp.bfloat16)
    grad_value = dot(probs_half, up, 0, 0)
    grad_probs = dot(up, value, 1, 1)
    inner = jnp.sum(probs * grad_probs, axis=-1, keepdims=True)
    grad_scores = (probs * (grad_probs - inner) * factor).astype(jnp.bfloat16)
    grad_query = norm_grad(dot(grad_scores, key, 1, 0), query_hat, query_inv, gain_query)
    grad_key = norm_grad(dot(grad_scores, query, 0, 0), key_hat, key_inv, gain_key)
    grads = (grad_query, grad_key, grad_value)
    return out, [part.astype(jnp.bfloat16) for part in grads]


def heads_kernel(
    order, own, other, weight, gain_q, gain_k, seg_col, seg_row, upstream, out, top, bottom, total
):
    size = gain_q.shape[-1]
    heads = gain_q.shape[0]
    half = top.shape[0]
    step, blocks = pl.program_id(0), pl.num_programs(0)

    @pl.when(step == 0)
    def _():
        total[...] = jnp.zeros_like(total)

    @pl.when(step < blocks // 2)
    def _():
        total[...] += dot(own[0], weight[...], 1, 0)

    @pl.when(step >= blocks // 2)
    def _():
        total[...] += dot(other[0], weight[...], 1, 0)

    @pl.when(step == blocks - 1)
    def _():
        for head in range(heads):
            left = 3 * head * size
            result, parts = attend(
                total[:, left : left + 3 * size], gain_q[head], gain_k[head],
                seg_col[...], seg_row[...], upstream[:, head * size : (head + 1) * size],
            )
            out[:, head * size : (head + 1) * size] = result
            for kind, part in enumerate(parts):
                span = slice(left + kind * size, left + (kind + 1) * size)
                top[:, span], bottom[:, span] = part[:half], part[half:]


def run_heads(order, own, other, weight, gain_query, gain_key, segments, upstream):
    heads, size = gain_query.shape
    rows = segments.shape[0]
    depth, cols = weight.shape
    blocks = order.shape[0]
    half = blocks // 2
    width = depth // blocks
    fixed = lambda step, order: (0, 0)
    cube = lambda step, order: (0, 0, 0)
    return pl.pallas_call(
        heads_kernel,
        out_shape=(
            jax.ShapeDtypeStruct((rows, heads * size), jnp.bfloat16),
            jax.ShapeDtypeStruct((rows // 2, cols), jnp.bfloat16),
            jax.ShapeDtypeStruct((rows // 2, cols), jnp.bfloat16),
        ),
        grid_spec=pltpu.PrefetchScalarGridSpec(
            num_scalar_prefetch=1,
            grid=(blocks,),
            in_specs=[
                pl.BlockSpec(
                    (1, rows, width), lambda step, order: (jnp.minimum(step, half - 1), 0, 0)
                ),
                pl.BlockSpec(
                    (1, rows, width), lambda step, order: (jnp.maximum(step - half, 0), 0, 0)
                ),
                pl.BlockSpec((width, cols), lambda step, order: (order[step], 0)),
                pl.BlockSpec((heads, 1, size), cube),
                pl.BlockSpec((heads, 1, size), cube),
                pl.BlockSpec((rows, 1), fixed),
                pl.BlockSpec((1, rows), fixed),
                pl.BlockSpec((rows, heads * size), fixed),
            ],
            out_specs=(
                pl.BlockSpec((rows, heads * size), fixed),
                pl.BlockSpec((rows // 2, cols), fixed),
                pl.BlockSpec((rows // 2, cols), fixed),
            ),
            scratch_shapes=[pltpu.VMEM((rows, cols), jnp.float32)],
        ),
        compiler_params=pltpu.CompilerParams(vmem_limit_bytes=VMEM_BYTES),
        cost_estimate=pl.CostEstimate(
            flops=2 * rows * depth * cols,
            bytes_accessed=2 * depth * cols + 2 * rows * depth,
            transcendentals=heads * rows * rows,
        ),
    )(
        order, own, other, weight, gain_query[:, None, :], gain_key[:, None, :],
        segments[:, None], segments[None, :], upstream,
    )


def weigh_near_kernel(table, low, high, *refs):
    grads, terms = refs[:-1], refs[-1]
    half = grads[0].shape[0]
    total = 0.0
    for sequence, rows in enumerate((low[0, 0], low[0, 1], high[0, 0])):
        top, bottom = grads[2 * sequence : 2 * sequence + 2]
        total += dot(rows[:half], top[...], 0, 0) + dot(rows[half:], bottom[...], 0, 0)
    terms[0] = total


def weigh_near(table, shared, grads):
    _, count, length, width = shared.shape
    pieces, cols = table.shape[0], grads[0].shape[1]
    return pl.pallas_call(
        weigh_near_kernel,
        out_shape=jax.ShapeDtypeStruct((pieces, width, cols), jnp.float32),
        grid_spec=pltpu.PrefetchScalarGridSpec(
            num_scalar_prefetch=1,
            grid=(pieces,),
            in_specs=[
                pl.BlockSpec(
                    (1, count, length, width), lambda piece, table: (2 * table[piece], 0, 0, 0)
                ),
                pl.BlockSpec(
                    (1, 1, length, width), lambda piece, table: (2 * table[piece] + 1, 0, 0, 0)
                ),
            ]
            + [pl.BlockSpec(grad.shape, lambda piece, table: (0, 0)) for grad in grads],
            out_specs=pl.BlockSpec((1, width, cols), lambda piece, table: (piece, 0, 0)),
        ),
        compiler_params=pltpu.CompilerParams(vmem_limit_bytes=VMEM_BYTES),
        cost_estimate=pl.CostEstimate(
            flops=6 * pieces * length * width * cols,
            bytes_accessed=4 * count * length * (pieces * width + cols),
            transcendentals=0,
        ),
    )(table, shared, shared, *grads)


def weigh_far_kernel(table, partial, rows, far_up, far_down, top, bottom):
    half = far_up.shape[0]
    total = partial[0] + dot(rows[0, 0, :half], far_up[...], 0, 0)
    total = (total + dot(rows[0, 0, half:], far_down[...], 0, 0)).astype(jnp.bfloat16)
    half = top.shape[1]
    top[0], bottom[0] = total[:half], total[half:]


def weigh_far(table, partial, shared, grads, start, stop):
    _, _, length, width = shared.shape
    cols = partial.shape[2]
    half = (1, width // 2, cols)
    out = jax.ShapeDtypeStruct((stop - start,) + half[1:], jnp.bfloat16)
    return pl.pallas_call(
        weigh_far_kernel,
        out_shape=(out, out),
        grid_spec=pltpu.PrefetchScalarGridSpec(
            num_scalar_prefetch=1,
            grid=(stop - start,),
            in_specs=[
                pl.BlockSpec((1, width, cols), lambda piece, table: (start + piece, 0, 0)),
                pl.BlockSpec(
                    (1, 1, length, width),
                    lambda piece, table: (2 * table[start + piece] + 1, 1, 0, 0),
                ),
            ]
            + [pl.BlockSpec(grad.shape, lambda piece, table: (0, 0)) for grad in grads],
            out_specs=(pl.BlockSpec(half, lambda piece, table: (piece, 0, 0)),) * 2,
        ),
        compiler_params=pltpu.CompilerParams(vmem_limit_bytes=VMEM_BYTES),
        cost_estimate=pl.CostEstimate(
            flops=2 * (stop - start) * length * width * cols,
            bytes_accessed=(stop - start) * width * (6 * cols + 4 * length),
            transcendentals=0,
        ),
    )(table, partial, shared, *grads)


def terms_kernel(top, bottom, weight, terms):
    half = top.shape[0]
    terms[:half] = dot(top[...], weight[...], 1, 1).astype(jnp.bfloat16)
    terms[half:] = dot(bottom[...], weight[...], 1, 1).astype(jnp.bfloat16)


def row_terms(grads, weight):
    half = grads[0].shape
    rows = 2 * half[0]
    depth, cols = weight.shape
    width = depth // 8
    return pl.pallas_call(
        terms_kernel,
        out_shape=jax.ShapeDtypeStruct((rows, depth), jnp.bfloat16),
        grid=(depth // width,),
        in_specs=[
            pl.BlockSpec(half, lambda block: (0, 0)),
            pl.BlockSpec(half, lambda block: (0, 0)),
            pl.BlockSpec((width, cols), lambda block: (block, 0)),
        ],
        out_specs=pl.BlockSpec((rows, width), lambda block: (0, block)),
        compiler_params=pltpu.CompilerParams(vmem_limit_bytes=VMEM_BYTES),
        cost_estimate=pl.CostEstimate(
            flops=2 * rows * depth * cols,
            bytes_accessed=2 * (rows * cols + depth * (cols + rows)),
            transcendentals=0,
        ),
    )(*grads, weight)


def total_of(*terms):
    return sum(term.astype(jnp.float32) for term in terms).astype(jnp.bfloat16)


def ring_near(block, send):
    return send(block, 1), send(block, -1)


def ring_far(before, after, send):
    half = before.shape[0] // 2
    return send(before[:half], 1), send(after[half:], -1)


def shards(loader_rows, packing, segment_ids, qkv_weight, gain_query, gain_key, out_grad):
    owners = lax.axis_size("row")
    block_count, block_rows, feature_cols = loader_rows.shape
    weight_panel = lax.all_gather(qkv_weight, "row", axis=0, tiled=True)

    col, row = lax.axis_index("col"), lax.axis_index("row")
    y, core = col // 2, col % 2
    x, z = row // N_RING, row % N_RING
    outgoing = pack_blocks(packing, loader_rows, owners)
    arrived = lax.all_to_all(outgoing, "row", split_axis=0, concat_axis=0, tiled=True)
    own_rows = place_blocks(arrived, block_count)
    own_rows = own_rows.reshape(block_count * block_rows, feature_cols)

    half = feature_cols // 2
    left, right = own_rows[:, :half], own_rows[:, half:]
    same, change = jnp.where(z % 2 == 0, left, right), jnp.where(z % 2 == 0, right, left)
    near = ring_near(own_rows, send_y)
    shared = [same, *ring_near(change, send_to_half), send_to_half(same, 2)]
    near, shared = lax.optimization_barrier((near, shared))

    low, high = jnp.stack(shared[:2]), jnp.stack(shared[2:])
    share = jnp.where(
        core == z // 2,
        jnp.where(core == 0, low, high),
        swap_core(jnp.where(core == 0, high, low)),
    )
    far = jnp.concatenate(ring_far(*near, send_y), axis=0)
    far, share = lax.optimization_barrier((far, share))
    own = jnp.stack([own_rows, *near, far])
    other = swap_core(own)
    shared = lax.all_gather(share, "col", axis=0)

    offsets = jnp.array([0, -1, 1, 2], jnp.int32)
    ys = (y + offsets) % N_RING
    order = jnp.concatenate([ys * 2 + core, ys * 2 + 1 - core]).astype(jnp.int32)
    table = ((x - offsets) % N_RING).astype(jnp.int32)
    attn_out, top, bottom = run_heads(
        order, own, other, weight_panel, gain_query, gain_key, segment_ids[0], out_grad
    )

    before_top, after_bottom = send_z(top, 1), send_z(bottom, -1)
    before_bottom, after_top = send_z(bottom, 1), send_z(top, -1)
    near, row_sums = lax.optimization_barrier(
        (
            [before_top, before_bottom, after_top, after_bottom],
            row_terms((top, bottom), weight_panel),
        )
    )
    far, partial = lax.optimization_barrier(
        (
            (send_z(before_top, 1), send_z(after_bottom, -1)),
            weigh_near(table, shared, [top, bottom, *near]),
        )
    )
    tops, bottoms = weigh_far(table, partial, shared, far, 3, 4)
    up, down = send_x(tops[0], 1), send_x(bottoms[0], -1)
    tops, bottoms = weigh_far(table, partial, shared, far, 0, 3)
    after = jnp.concatenate([total_of(tops[1], up), bottoms[1]], axis=0)
    before = jnp.concatenate([tops[2], total_of(bottoms[2], down)], axis=0)
    here = jnp.concatenate([tops[0], bottoms[0]], axis=0)
    grad_weight = total_of(here, send_x(after, 1), send_x(before, -1))
    grad_rows = lax.psum_scatter(row_sums, "col", scatter_dimension=1, tiled=True)
    return (attn_out, grad_rows, grad_weight)


def solution(mesh):
    in_specs = (
        P("row", None, "col"),
        P("row"),
        P("row", None),
        P("row", "col"),
        P("col", None),
        P("col", None),
        P("row", "col"),
    )
    out_specs = (P("row", "col"), P("row", "col"), P("row", "col"))
    return jax.shard_map(shards, mesh=mesh, in_specs=in_specs, out_specs=out_specs, check_vma=False)
```

profile of v0, /device:TPU:6, one launch (start us, length us, event | category | flops | bytes accessed | tf_op | source)
XLA Modules:
  0.0 247.7 jit_solution(986190031926170476)
XLA Ops:
  7.9 2.9 %shard_map.103 = bf16[16,32,1664]{2,1,0:T(8,128)(2,1)} custom-call(s32[16]{0:T(128)} %packing.1, bf16[16,32,768]{2,1,0:T(8,128)(2,1)} %blocks.1), custom_call_target="tpu_custom_call" | custom-call | tf_op jit(solution)/shard_map/pallas_call | solution.py:91
  10.9 44.3 %all_to_all.5.arrived = bf16[16,32,1664]{2,1,0:T(8,128)(2,1)S(1)} all-to-all(bf16[16,32,1664]{2,1,0:T(8,128)(2,1)} %shard_map.103), channel_id=1, replica_groups=mesh['row'=16,'col'=8] {'row'}, dimensions={0} | all-to-all | bytes 3407872 | tf_op jit(solution)/shard_map/all_to_all | solution.py:397
  56.4 2.6 %shard_map.104 = bf16[16,32,768]{2,1,0:T(8,128)(2,1)} custom-call(s32[16]{0:T(128)} %select_reduce_fusion.where, bf16[16,32,1664]{2,1,0:T(8,128)(2,1)} %copy-done.1), custom_call_target="tpu_custom_call" | custom-call | tf_op jit(solution)/shard_map/pallas_call | solution.py:128
  59.0 1.6 collective-permute-start
  60.6 1.7 collective-permute-start.1
  63.7 2.2 collective-permute-start.2
  68.5 18.6 %collective-permute-done.2 = bf16[512,384]{1,0:T(8,128)(2,1)S(1)} collective-permute-done((bf16[512,384]{1,0:T(8,128)(2,1)S(1)}, bf16[512,384]{1,0:T(8,128)(2,1)S(1)}, u32[]{:S(2)}, u32[]{:S(2)}) %collective-permute-start.2) | collective-permute-done | bytes 393248 | tf_op jit(solution)/shard_map/ppermute | solution.py:48
  89.4 3.2 %collective-permute-start.6 = (bf16[256,768]{1,0:T(8,128)(2,1)}, bf16[256,768]{1,0:T(8,128)(2,1)}, u32[]{:S(2)}, u32[]{:S(2)}) collective-permute-start(bf16[256,768]{1,0:T(8,128)(2,1)} %slice.37), channel_id=1, source_target_pairs={{0,6},{1,7},{2,0},{3,1},{4,2},{5,3},{6,4},{7,5},{8,14},{9,15},{10,... | collective-permute-start | bytes 1179656 | tf_op jit(solution)/shard_map/ppermute | solution.py:37
  92.6 8.8 %collective-permute-done.5 = bf16[256,768]{1,0:T(8,128)(2,1)} collective-permute-done((bf16[256,768]{1,0:T(8,128)(2,1)S(1)}, bf16[256,768]{1,0:T(8,128)(2,1)}, u32[]{:S(2)}, u32[]{:S(2)}) %collective-permute-start.5) | collective-permute-done | bytes 393248 | tf_op jit(solution)/shard_map/ppermute | solution.py:37
  104.1 1.9 pad_maximum_fusion.own
  109.3 2.9 %collective-permute-done.8.other = bf16[4,512,768]{2,1,0:T(8,128)(2,1)} collective-permute-done((bf16[4,512,768]{2,1,0:T(8,128)(2,1)}, bf16[4,512,768]{2,1,0:T(8,128)(2,1)}, u32[]{:S(2)}, u32[]{:S(2)}) %collective-permute-start.8) | collective-permute-done | bytes 3145760 | tf_op jit(solution)/shard_map/ppermute | solution.py:52
  112.2 19.6 %all-gather.4.cloned.1.call-done.weight = bf16[6144,1152]{1,0:T(8,128)(2,1)} async-done(((bf16[384,1152]{1,0:T(8,128)(2,1)}), bf16[6144,1152]{1,0:T(8,128)(2,1)}) %all-gather.4.cloned.1.call-update) | async-done | bytes 14155792 | tf_op jit(solution)/shard_map/all_gather | solution.py:391
  131.9 22.5 %shard_map.105 = (bf16[512,384]{1,0:T(8,128)(2,1)}, bf16[256,1152]{1,0:T(8,128)(2,1)}, bf16[256,1152]{1,0:T(8,128)(2,1)}) custom-call(s32[8]{0:T(128)} %pad_add_fusion.order, bf16[4,512,768]{2,1,0:T(8,128)(2,1)} %pad_maximum_fusion.own, bf16[4,512,768]{2,1,0:T(8,128)(2,1)} %collective-permute-done.8.other, ...), custom_call_target="tpu_custom_call" | custom-call | flops 7247757312 | bytes 20447232 | tf_op jit(solution)/shard_map/pallas_call | solution.py:225
  154.3 3.2 %collective-permute-start.12 = (bf16[256,1152]{1,0:T(8,128)(2,1)}, bf16[256,1152]{1,0:T(8,128)(2,1)S(1)}, u32[]{:S(2)}, u32[]{:S(2)}) collective-permute-start(bf16[256,1152]{1,0:T(8,128)(2,1)} %get-tuple-element.35.bottom.refs_1_), channel_id=1, source_target_pairs={{0,24},{8,0},{16,8},{24,16},{32,56},{40,32},{48,40},{56,48},{64,88... | collective-permute-start | bytes 1769480 | tf_op jit(solution)/shard_map/ppermute | solution.py:33
  157.6 2.0 collective-permute-start.9
  159.6 14.7 %shard_map.106 = bf16[512,6144]{1,0:T(8,128)(2,1)} custom-call(bf16[256,1152]{1,0:T(8,128)(2,1)} %get-tuple-element.34.top.refs_0_, bf16[256,1152]{1,0:T(8,128)(2,1)} %get-tuple-element.35.bottom.refs_1_, bf16[6144,1152]{1,0:T(8,128)(2,1)} %all-gather.4.cloned.1.call-done.weight), custom_call_target="tpu_custom_call" | custom-call | flops 7247757312 | bytes 21626880 | tf_op jit(solution)/shard_map/pallas_call | solution.py:356
  174.3 8.2 %collective-permute-done.11.refs_4_ = bf16[256,1152]{1,0:T(8,128)(2,1)S(1)} collective-permute-done((bf16[256,1152]{1,0:T(8,128)(2,1)}, bf16[256,1152]{1,0:T(8,128)(2,1)S(1)}, u32[]{:S(2)}, u32[]{:S(2)}) %collective-permute-start.11) | collective-permute-done | bytes 589856 | tf_op jit(solution)/shard_map/ppermute | solution.py:33
  184.1 3.5 %collective-permute-start.14 = (bf16[256,1152]{1,0:T(8,128)(2,1)S(1)}, bf16[256,1152]{1,0:T(8,128)(2,1)S(1)}, u32[]{:S(2)}, u32[]{:S(2)}) collective-permute-start(bf16[256,1152]{1,0:T(8,128)(2,1)S(1)} %collective-permute-done.12.refs_5_), channel_id=1, source_target_pairs={{0,24},{8,0},{16,8},{24,16},{32,56},{40,32},{48,40},{56,48},{64,88... | collective-permute-start | bytes 1769480 | tf_op jit(solution)/shard_map/ppermute | solution.py:33
  188.1 11.4 %shard_map.107.partial = f32[4,384,1152]{2,1,0:T(8,128)} custom-call(s32[4]{0:T(128)} %and_select_fusion.table, bf16[8,2,512,384]{3,2,1,0:T(8,128)(2,1)} %bitcast.27, bf16[8,2,512,384]{3,2,1,0:T(8,128)(2,1)} %bitcast.28, bf16[256,1152]{1,0:T(8,128)(2,1)} %get-tuple-element.34.top.refs_0_, bf16[256,1152]{1,0:T(8,128)(2,1)} %get-tuple-element.35.bottom.refs_1_, ...), custom_call_target="tpu_custom_call" | custom-call | flops 5435817984 | bytes 11010048 | tf_op jit(solution)/shard_map/pallas_call | solution.py:281
  201.2 4.2 %shard_map.109 = (bf16[1,192,1152]{2,1,0:T(8,128)(2,1)}, bf16[1,192,1152]{2,1,0:T(8,128)(2,1)}) custom-call(s32[4]{0:T(128)} %and_select_fusion.table, f32[4,384,1152]{2,1,0:T(8,128)} %shard_map.107.partial, bf16[8,2,512,384]{3,2,1,0:T(8,128)(2,1)} %bitcast.29, bf16[256,1152]{1,0:T(8,128)(2,1)} %copy-done.2, bf16[256,1152]{1,0:T(8,128)(2,1)} %copy-done.3), custom_call_target="tpu_custom_call" | custom-call | flops 452984832 | bytes 3440640 | tf_op jit(solution)/shard_map/pallas_call | solution.py:320
  207.4 7.1 %shard_map.108 = (bf16[3,192,1152]{2,1,0:T(8,128)(2,1)}, bf16[3,192,1152]{2,1,0:T(8,128)(2,1)}) custom-call(s32[4]{0:T(128)} %and_select_fusion.table, f32[4,384,1152]{2,1,0:T(8,128)} %shard_map.107.partial, bf16[8,2,512,384]{3,2,1,0:T(8,128)(2,1)} %bitcast.30, bf16[256,1152]{1,0:T(8,128)(2,1)} %copy-done.2, bf16[256,1152]{1,0:T(8,128)(2,1)} %copy-done.3), custom_call_target="tpu_custom_call" | custom-call | flops 1358954496 | bytes 10321920 | tf_op jit(solution)/shard_map/pallas_call | solution.py:320
  216.5 2.0 collective-permute-start.16
  219.8 15.8 %collective-permute-done.16 = bf16[384,1152]{1,0:T(8,128)(2,1)S(1)} collective-permute-done((bf16[384,1152]{1,0:T(8,128)(2,1)S(1)}, bf16[384,1152]{1,0:T(8,128)(2,1)S(1)}, u32[]{:S(2)}, u32[]{:S(2)}) %collective-permute-start.16) | collective-permute-done | bytes 884768 | tf_op jit(solution)/shard_map/ppermute | solution.py:29
  235.7 4.3 %collective-permute-done.18 = bf16[384,1152]{1,0:T(8,128)(2,1)S(1)} collective-permute-done((bf16[384,1152]{1,0:T(8,128)(2,1)S(1)}, bf16[384,1152]{1,0:T(8,128)(2,1)S(1)}, u32[]{:S(2)}, u32[]{:S(2)}) %collective-permute-start.18) | collective-permute-done | bytes 884768 | tf_op jit(solution)/shard_map/ppermute | solution.py:29
  (96 shorter events, 24.4 us)
Async XLA Ops:
  7.2 124.7 %all-gather.4.cloned.1.call-start = ((), (), s32[]{:S(2)}) async-start(), calls=%async_computation.2 | async-start | bytes 15040512 | tf_op jit(solution)/shard_map/all_gather | solution.py:391
  7.9 180.2 %all-gather.6.cloned.1.call-start = ((), (), s32[]{:S(2)}) async-start(), calls=%async_computation.4 | async-start | bytes 7077888 | tf_op jit(solution)/shard_map/all_gather | solution.py:418
  59.0 28.2 %collective-permute-start = (bf16[512,768]{1,0:T(8,128)(2,1)}, bf16[512,768]{1,0:T(8,128)(2,1)S(1)}, u32[]{:S(2)}, u32[]{:S(2)}) collective-permute-start(bf16[512,768]{1,0:T(8,128)(2,1)} %bitcast.31), channel_id=1, source_target_pairs={{0,2},{1,3},{2,4},{3,5},{4,6},{5,7},{6,0},{7,1},{8,10},{9,11},{10,... | collective-permute-start | bytes 2359304 | tf_op jit(solution)/shard_map/ppermute | solution.py:37
  60.6 26.6 %collective-permute-start.1 = (bf16[512,768]{1,0:T(8,128)(2,1)}, bf16[512,768]{1,0:T(8,128)(2,1)S(1)}, u32[]{:S(2)}, u32[]{:S(2)}) collective-permute-start(bf16[512,768]{1,0:T(8,128)(2,1)} %bitcast.32), channel_id=1, source_target_pairs={{0,6},{1,7},{2,0},{3,1},{4,2},{5,3},{6,4},{7,5},{8,14},{9,15},{10,... | collective-permute-start | bytes 2359304 | tf_op jit(solution)/shard_map/ppermute | solution.py:37
  63.7 23.5 %collective-permute-start.2 = (bf16[512,384]{1,0:T(8,128)(2,1)S(1)}, bf16[512,384]{1,0:T(8,128)(2,1)S(1)}, u32[]{:S(2)}, u32[]{:S(2)}) collective-permute-start(bf16[512,384]{1,0:T(8,128)(2,1)S(1)} %get-tuple-element.55), channel_id=1, source_target_pairs={{0,8},{2,10},{4,12},{6,14},{9,17},{11,19},{13,21},{15,23},{17,25},... | collective-permute-start | bytes 1179656 | tf_op jit(solution)/shard_map/ppermute | solution.py:48
  65.9 21.2 %collective-permute-start.3 = (bf16[512,384]{1,0:T(8,128)(2,1)S(1)}, bf16[512,384]{1,0:T(8,128)(2,1)S(1)}, u32[]{:S(2)}, u32[]{:S(2)}) collective-permute-start(bf16[512,384]{1,0:T(8,128)(2,1)S(1)} %get-tuple-element.55), channel_id=1, source_target_pairs={{1,25},{3,27},{5,29},{7,31},{8,0},{10,2},{12,4},{14,6},{16,8},{18,... | collective-permute-start | bytes 1179656 | tf_op jit(solution)/shard_map/ppermute | solution.py:48
  67.2 20.0 %collective-permute-start.4 = (bf16[512,384]{1,0:T(8,128)(2,1)S(1)}, bf16[512,384]{1,0:T(8,128)(2,1)S(1)}, u32[]{:S(2)}, u32[]{:S(2)}) collective-permute-start(bf16[512,384]{1,0:T(8,128)(2,1)S(1)} %get-tuple-element.28), channel_id=1, source_target_pairs={{1,17},{3,19},{5,21},{7,23},{9,25},{11,27},{13,29},{15,31},{16,0},... | collective-permute-start | bytes 1179656 | tf_op jit(solution)/shard_map/ppermute | solution.py:48
  88.4 14.4 %collective-permute-start.7 = (bf16[2,512,384]{2,1,0:T(8,128)(2,1)}, bf16[2,512,384]{2,1,0:T(8,128)(2,1)}, u32[]{:S(2)}, u32[]{:S(2)}) collective-permute-start(bf16[2,512,384]{2,1,0:T(8,128)(2,1)} %broadcast_select_fusion), channel_id=1, source_target_pairs={{0,1},{1,0},{2,3},{3,2},{4,5},{5,4},{6,7},{7,6},{8,9},{9,8},{10,11... | collective-permute-start | bytes 2359304 | tf_op jit(solution)/shard_map/ppermute | solution.py:52
  88.4 12.9 %collective-permute-start.5 = (bf16[256,768]{1,0:T(8,128)(2,1)S(1)}, bf16[256,768]{1,0:T(8,128)(2,1)}, u32[]{:S(2)}, u32[]{:S(2)}) collective-permute-start(bf16[256,768]{1,0:T(8,128)(2,1)S(1)} %slice.36), channel_id=1, source_target_pairs={{0,2},{1,3},{2,4},{3,5},{4,6},{5,7},{6,0},{7,1},{8,10},{9,11},{10,... | collective-permute-start | bytes 1179656 | tf_op jit(solution)/shard_map/ppermute | solution.py:37
  89.4 12.3 %collective-permute-start.6 = (bf16[256,768]{1,0:T(8,128)(2,1)}, bf16[256,768]{1,0:T(8,128)(2,1)}, u32[]{:S(2)}, u32[]{:S(2)}) collective-permute-start(bf16[256,768]{1,0:T(8,128)(2,1)} %slice.37), channel_id=1, source_target_pairs={{0,6},{1,7},{2,0},{3,1},{4,2},{5,3},{6,4},{7,5},{8,14},{9,15},{10,... | collective-permute-start | bytes 1179656 | tf_op jit(solution)/shard_map/ppermute | solution.py:37
  92.6 10.3 %copy-start.9 = (bf16[512,384]{1,0:T(8,128)(2,1)S(1)}, bf16[512,384]{1,0:T(8,128)(2,1)}, u32[]{:S(2)}) copy-start(bf16[512,384]{1,0:T(8,128)(2,1)} %copy-done.8) | copy-start | bytes 1179652
  104.0 137.2 %reduce-scatter.2.cloned.1.call-start = ((), (), s32[]{:S(2)}) async-start(), calls=%async_computation.3 | async-start | bytes 7077888 | tf_op jit(solution)/shard_map/reduce_scatter | solution.py:449
  106.0 6.2 %collective-permute-start.8 = (bf16[4,512,768]{2,1,0:T(8,128)(2,1)}, bf16[4,512,768]{2,1,0:T(8,128)(2,1)}, u32[]{:S(2)}, u32[]{:S(2)}) collective-permute-start(bf16[4,512,768]{2,1,0:T(8,128)(2,1)} %pad_maximum_fusion.own), channel_id=1, source_target_pairs={{0,1},{1,0},{2,3},{3,2},{4,5},{5,4},{6,7},{7,6},{8,9},{9,8},{10,11... | collective-permute-start | bytes 9437192 | tf_op jit(solution)/shard_map/ppermute | solution.py:52
  154.3 20.0 %collective-permute-start.10 = (bf16[256,1152]{1,0:T(8,128)(2,1)}, bf16[256,1152]{1,0:T(8,128)(2,1)S(1)}, u32[]{:S(2)}, u32[]{:S(2)}) collective-permute-start(bf16[256,1152]{1,0:T(8,128)(2,1)} %get-tuple-element.35.bottom.refs_1_), channel_id=1, source_target_pairs={{0,8},{8,16},{16,24},{24,0},{32,40},{40,48},{48,56},{56,32},{64,72... | collective-permute-start | bytes 1769480 | tf_op jit(solution)/shard_map/ppermute | solution.py:33
  154.3 28.2 %collective-permute-start.12 = (bf16[256,1152]{1,0:T(8,128)(2,1)}, bf16[256,1152]{1,0:T(8,128)(2,1)S(1)}, u32[]{:S(2)}, u32[]{:S(2)}) collective-permute-start(bf16[256,1152]{1,0:T(8,128)(2,1)} %get-tuple-element.35.bottom.refs_1_), channel_id=1, source_target_pairs={{0,24},{8,0},{16,8},{24,16},{32,56},{40,32},{48,40},{56,48},{64,88... | collective-permute-start | bytes 1769480 | tf_op jit(solution)/shard_map/ppermute | solution.py:33
  157.6 25.0 %collective-permute-start.11 = (bf16[256,1152]{1,0:T(8,128)(2,1)}, bf16[256,1152]{1,0:T(8,128)(2,1)S(1)}, u32[]{:S(2)}, u32[]{:S(2)}) collective-permute-start(bf16[256,1152]{1,0:T(8,128)(2,1)} %get-tuple-element.34.top.refs_0_), channel_id=1, source_target_pairs={{0,24},{8,0},{16,8},{24,16},{32,56},{40,32},{48,40},{56,48},{64,88... | collective-permute-start | bytes 1769480 | tf_op jit(solution)/shard_map/ppermute | solution.py:33
  157.6 25.6 %collective-permute-start.9 = (bf16[256,1152]{1,0:T(8,128)(2,1)}, bf16[256,1152]{1,0:T(8,128)(2,1)S(1)}, u32[]{:S(2)}, u32[]{:S(2)}) collective-permute-start(bf16[256,1152]{1,0:T(8,128)(2,1)} %get-tuple-element.34.top.refs_0_), channel_id=1, source_target_pairs={{0,8},{8,16},{16,24},{24,0},{32,40},{40,48},{48,56},{56,32},{64,72... | collective-permute-start | bytes 1769480 | tf_op jit(solution)/shard_map/ppermute | solution.py:33
  174.3 13.2 %copy-start.19 = (s32[4]{0:T(128)S(1)}, s32[4]{0:T(128)}, u32[]{:S(2)}) copy-start(s32[4]{0:T(128)} %constant.86) | copy-start | bytes 52
  184.1 15.5 %collective-permute-start.13 = (bf16[256,1152]{1,0:T(8,128)(2,1)S(1)}, bf16[256,1152]{1,0:T(8,128)(2,1)S(1)}, u32[]{:S(2)}, u32[]{:S(2)}) collective-permute-start(bf16[256,1152]{1,0:T(8,128)(2,1)S(1)} %collective-permute-done.9.refs_2_), channel_id=1, source_target_pairs={{0,8},{8,16},{16,24},{24,0},{32,40},{40,48},{48,56},{56,32},{64,72... | collective-permute-start | bytes 1769480 | tf_op jit(solution)/shard_map/ppermute | solution.py:33
  184.1 15.5 %collective-permute-start.14 = (bf16[256,1152]{1,0:T(8,128)(2,1)S(1)}, bf16[256,1152]{1,0:T(8,128)(2,1)S(1)}, u32[]{:S(2)}, u32[]{:S(2)}) collective-permute-start(bf16[256,1152]{1,0:T(8,128)(2,1)S(1)} %collective-permute-done.12.refs_5_), channel_id=1, source_target_pairs={{0,24},{8,0},{16,8},{24,16},{32,56},{40,32},{48,40},{56,48},{64,88... | collective-permute-start | bytes 1769480 | tf_op jit(solution)/shard_map/ppermute | solution.py:33
  205.4 10.9 %collective-permute-start.15 = (bf16[192,1152]{1,0:T(8,128)(2,1)}, bf16[192,1152]{1,0:T(8,128)(2,1)S(1)}, u32[]{:S(2)}, u32[]{:S(2)}) collective-permute-start(bf16[192,1152]{1,0:T(8,128)(2,1)} %bitcast.48), channel_id=1, source_target_pairs={{0,32},{8,40},{16,48},{24,56},{32,64},{40,72},{48,80},{56,88},{64,... | collective-permute-start | bytes 1327112 | tf_op jit(solution)/shard_map/ppermute | solution.py:29
  206.1 12.3 %collective-permute-start.17 = (bf16[192,1152]{1,0:T(8,128)(2,1)}, bf16[192,1152]{1,0:T(8,128)(2,1)S(1)}, u32[]{:S(2)}, u32[]{:S(2)}) collective-permute-start(bf16[192,1152]{1,0:T(8,128)(2,1)} %bitcast.47), channel_id=1, source_target_pairs={{0,96},{8,104},{16,112},{24,120},{32,0},{40,8},{48,16},{56,24},{64... | collective-permute-start | bytes 1327112 | tf_op jit(solution)/shard_map/ppermute | solution.py:29
  216.5 19.2 %collective-permute-start.16 = (bf16[384,1152]{1,0:T(8,128)(2,1)S(1)}, bf16[384,1152]{1,0:T(8,128)(2,1)S(1)}, u32[]{:S(2)}, u32[]{:S(2)}) collective-permute-start(bf16[384,1152]{1,0:T(8,128)(2,1)S(1)} %pad_maximum_fusion.1), channel_id=1, source_target_pairs={{0,32},{8,40},{16,48},{24,56},{32,64},{40,72},{48,80},{56,88},{64,... | collective-permute-start | bytes 2654216 | tf_op jit(solution)/shard_map/ppermute | solution.py:29
  219.7 20.3 %collective-permute-start.18 = (bf16[384,1152]{1,0:T(8,128)(2,1)S(1)}, bf16[384,1152]{1,0:T(8,128)(2,1)S(1)}, u32[]{:S(2)}, u32[]{:S(2)}) collective-permute-start(bf16[384,1152]{1,0:T(8,128)(2,1)S(1)} %pad_maximum_fusion.2), channel_id=1, source_target_pairs={{0,96},{8,104},{16,112},{24,120},{32,0},{40,8},{48,16},{56,24},{64... | collective-permute-start | bytes 2654216 | tf_op jit(solution)/shard_map/ppermute | solution.py:29
  (18 other events, 59.7 us)
Sparse Core Ops, SparseCore 0:
  10.2 121.6 all-gather.3
  134.1 39.8 all-gather.5
  183.4 43.6 reduce-scatter.1
where the time goes:
time: 249 us; the launch traced here: 248 us
  waiting for transfers between devices  79.9 us (32%)
  Pallas kernels  65.5 us (26%)
  blocking collectives  44.3 us (18%)
  starting transfers between devices  25.1 us (10%)
  between operations  14 us (6%)
  other arithmetic  11.6 us (5%)
  local copies, waits for them, and re-layouts  7.26 us (3%)
    all_to_all x1, blocking collectives, shards(): lax.all_to_all(outgoing, 'row', split_axis=0, concat_axis=0, tiled=True)  44.3 us
    pallas_call x1, Pallas kernels, run_heads(): pl.pallas_call(heads_kernel, out_shape=(jax.ShapeDtypeStruct((rows, heads...  22.5 us
    ppermute x4, waiting for transfers between devices, send_x(): return lax.ppermute(values, 'row', along_row(step, 0))  20.1 us
    all_gather x1, waiting for transfers between devices, shards(): weight_panel = lax.all_gather(qkv_weight, 'row', axis=0, tiled=True)  19.6 us
    ppermute x3, waiting for transfers between devices, send_to_half(): return lax.ppermute(values, ('row', 'col'), pairs)  18.6 us
    pallas_call x1, Pallas kernels, row_terms(): pl.pallas_call(terms_kernel, out_shape=jax.ShapeDtypeStruct((rows, depth)...  14.7 us
    pallas_call x1, Pallas kernels, weigh_near(): pl.pallas_call(weigh_near_kernel, out_shape=jax.ShapeDtypeStruct((pieces,...  11.4 us
    pallas_call x2, Pallas kernels, weigh_far(): pl.pallas_call(weigh_far_kernel, out_shape=(out, out), grid_spec=pltpu.Pr...  11.3 us
  transfers between devices with their start and end apart: 22, of which 9 were waited for; matrix products, arithmetic and copies ran while one was open for 6% of the time, Pallas kernels for 26%

commit v1 on v0

--- a/solution.py
+++ b/solution.py
@@ -9,6 +9,7 @@
 N_RING = 4
 LABEL_COLS = 128
 VMEM_BYTES = 56 * 1024 * 1024
+SMALL_VMEM_BYTES = 32 * 1024 * 1024
 
 
 def along_col(dy, dc):
@@ -295,7 +296,7 @@
             + [pl.BlockSpec(grad.shape, lambda piece, table: (0, 0)) for grad in grads],
             out_specs=pl.BlockSpec((1, width, cols), lambda piece, table: (piece, 0, 0)),
         ),
-        compiler_params=pltpu.CompilerParams(vmem_limit_bytes=VMEM_BYTES),
+        compiler_params=pltpu.CompilerParams(vmem_limit_bytes=SMALL_VMEM_BYTES),
         cost_estimate=pl.CostEstimate(
             flops=6 * pieces * length * width * cols,
             bytes_accessed=4 * count * length * (pieces * width + cols),
@@ -333,7 +334,7 @@
             + [pl.BlockSpec(grad.shape, lambda piece, table: (0, 0)) for grad in grads],
             out_specs=(pl.BlockSpec(half, lambda piece, table: (piece, 0, 0)),) * 2,
         ),
-        compiler_params=pltpu.CompilerParams(vmem_limit_bytes=VMEM_BYTES),
+        compiler_params=pltpu.CompilerParams(vmem_limit_bytes=SMALL_VMEM_BYTES),
         cost_estimate=pl.CostEstimate(
             flops=2 * (stop - start) * length * width * cols,
             bytes_accessed=(stop - start) * width * (6 * cols + 4 * length),

time: 249 us -> 243 us (0.976)
  Pallas kernels: 65.5 us -> 56.3 us
  waiting for transfers between devices: 79.9 us -> 84.1 us
    pallas_call x2, Pallas kernels: 11.3 us -> 3.94 us  [weigh_far(): pl.pallas_call(weigh_far_kernel, out_shape=(out, out), grid_spec=pltpu.Pr...]
    ppermute x4, waiting for transfers between devices: 20.1 us -> 24.1 us  [send_x(): return lax.ppermute(values, 'row', along_row(step, 0))]
    unnamed x40 -> x42, local copies, waits for them, and re-layouts: 2.84 us -> 5.1 us
  transfers between devices with their start and end apart: 22 -> 22, of which waited for: 9 -> 10; matrix products, arithmetic and copies ran while one was open for 6% -> 5% of each run, Pallas kernels for 26% -> 23%
where the time goes in v1:
time: 243 us; the launch traced here: 242 us
  waiting for transfers between devices  84.1 us (35%)
  Pallas kernels  56.3 us (23%)
  blocking collectives  44.3 us (18%)
  starting transfers between devices  25.3 us (10%)
  between operations  14.1 us (6%)
  other arithmetic  9.99 us (4%)
  local copies, waits for them, and re-layouts  8.23 us (3%)
    all_to_all x1, blocking collectives, shards(): lax.all_to_all(outgoing, 'row', split_axis=0, concat_axis=0, tiled=True)  44.3 us
    ppermute x4, waiting for transfers between devices, send_x(): return lax.ppermute(values, 'row', along_row(step, 0))  24.1 us
    pallas_call x1, Pallas kernels, run_heads(): pl.pallas_call(heads_kernel, out_shape=(jax.ShapeDtypeStruct((rows, heads...  22.5 us
    all_gather x1, waiting for transfers between devices, shards(): weight_panel = lax.all_gather(qkv_weight, 'row', axis=0, tiled=True)  19.6 us
    ppermute x3, waiting for transfers between devices, send_to_half(): return lax.ppermute(values, ('row', 'col'), pairs)  18.6 us
    pallas_call x1, Pallas kernels, row_terms(): pl.pallas_call(terms_kernel, out_shape=jax.ShapeDtypeStruct((rows, depth)...  14.7 us
    pallas_call x1, Pallas kernels, weigh_near(): pl.pallas_call(weigh_near_kernel, out_shape=jax.ShapeDtypeStruct((pieces,...  9.63 us
    ppermute x4, waiting for transfers between devices, send_y(): return lax.ppermute(values, 'col', along_col(step, 0))  9.08 us
  transfers between devices with their start and end apart: 22, of which 10 were waited for; matrix products, arithmetic and copies ran while one was open for 5% of the time, Pallas kernels for 23%

profile of v1, /device:TPU:6, one launch (start us, length us, event | category | flops | bytes accessed | tf_op | source)
XLA Modules:
  0.0 242.3 jit_solution(13928109009636778362)
XLA Ops:
  7.9 2.9 %shard_map.103 = bf16[16,32,1664]{2,1,0:T(8,128)(2,1)} custom-call(s32[16]{0:T(128)} %packing.1, bf16[16,32,768]{2,1,0:T(8,128)(2,1)} %blocks.1), custom_call_target="tpu_custom_call" | custom-call | tf_op jit(solution)/shard_map/pallas_call | solution.py:92
  10.9 44.3 %all_to_all.5.arrived = bf16[16,32,1664]{2,1,0:T(8,128)(2,1)S(1)} all-to-all(bf16[16,32,1664]{2,1,0:T(8,128)(2,1)} %shard_map.103), channel_id=1, replica_groups=mesh['row'=16,'col'=8] {'row'}, dimensions={0} | all-to-all | bytes 3407872 | tf_op jit(solution)/shard_map/all_to_all | solution.py:398
  56.4 2.6 %shard_map.104 = bf16[16,32,768]{2,1,0:T(8,128)(2,1)} custom-call(s32[16]{0:T(128)} %select_reduce_fusion.where, bf16[16,32,1664]{2,1,0:T(8,128)(2,1)} %copy-done.9), custom_call_target="tpu_custom_call" | custom-call | tf_op jit(solution)/shard_map/pallas_call | solution.py:129
  60.6 1.7 collective-permute-start.1
  63.7 2.2 collective-permute-start.2
  68.5 18.6 %collective-permute-done.2 = bf16[512,384]{1,0:T(8,128)(2,1)S(1)} collective-permute-done((bf16[512,384]{1,0:T(8,128)(2,1)S(1)}, bf16[512,384]{1,0:T(8,128)(2,1)S(1)}, u32[]{:S(2)}, u32[]{:S(2)}) %collective-permute-start.2) | collective-permute-done | bytes 393248 | tf_op jit(solution)/shard_map/ppermute | solution.py:49
  89.4 3.2 %collective-permute-start.6 = (bf16[256,768]{1,0:T(8,128)(2,1)}, bf16[256,768]{1,0:T(8,128)(2,1)}, u32[]{:S(2)}, u32[]{:S(2)}) collective-permute-start(bf16[256,768]{1,0:T(8,128)(2,1)} %slice.37), channel_id=1, source_target_pairs={{0,6},{1,7},{2,0},{3,1},{4,2},{5,3},{6,4},{7,5},{8,14},{9,15},{10,... | collective-permute-start | bytes 1179656 | tf_op jit(solution)/shard_map/ppermute | solution.py:38
  92.6 8.8 %collective-permute-done.5 = bf16[256,768]{1,0:T(8,128)(2,1)} collective-permute-done((bf16[256,768]{1,0:T(8,128)(2,1)S(1)}, bf16[256,768]{1,0:T(8,128)(2,1)}, u32[]{:S(2)}, u32[]{:S(2)}) %collective-permute-start.5) | collective-permute-done | bytes 393248 | tf_op jit(solution)/shard_map/ppermute | solution.py:38
  104.1 1.9 pad_maximum_fusion.own
  109.3 2.9 %collective-permute-done.8.other = bf16[4,512,768]{2,1,0:T(8,128)(2,1)} collective-permute-done((bf16[4,512,768]{2,1,0:T(8,128)(2,1)}, bf16[4,512,768]{2,1,0:T(8,128)(2,1)}, u32[]{:S(2)}, u32[]{:S(2)}) %collective-permute-start.8) | collective-permute-done | bytes 3145760 | tf_op jit(solution)/shard_map/ppermute | solution.py:53
  112.2 19.6 %all-gather.4.cloned.1.call-done.weight = bf16[6144,1152]{1,0:T(8,128)(2,1)} async-done(((bf16[384,1152]{1,0:T(8,128)(2,1)}), bf16[6144,1152]{1,0:T(8,128)(2,1)}) %all-gather.4.cloned.1.call-update) | async-done | bytes 14155792 | tf_op jit(solution)/shard_map/all_gather | solution.py:392
  131.9 22.5 %shard_map.105 = (bf16[512,384]{1,0:T(8,128)(2,1)}, bf16[256,1152]{1,0:T(8,128)(2,1)}, bf16[256,1152]{1,0:T(8,128)(2,1)}) custom-call(s32[8]{0:T(128)} %pad_add_fusion.order, bf16[4,512,768]{2,1,0:T(8,128)(2,1)} %pad_maximum_fusion.own, bf16[4,512,768]{2,1,0:T(8,128)(2,1)} %collective-permute-done.8.other, ...), custom_call_target="tpu_custom_call" | custom-call | flops 7247757312 | bytes 20447232 | tf_op jit(solution)/shard_map/pallas_call | solution.py:226
  154.3 3.2 %collective-permute-start.12 = (bf16[256,1152]{1,0:T(8,128)(2,1)}, bf16[256,1152]{1,0:T(8,128)(2,1)}, u32[]{:S(2)}, u32[]{:S(2)}) collective-permute-start(bf16[256,1152]{1,0:T(8,128)(2,1)} %get-tuple-element.35.bottom.refs_1_), channel_id=1, source_target_pairs={{0,24},{8,0},{16,8},{24,16},{32,56},{40,32},{48,40},{56,48},{64,88... | collective-permute-start | bytes 1769480 | tf_op jit(solution)/shard_map/ppermute | solution.py:34
  157.6 2.0 collective-permute-start.9
  159.6 14.7 %shard_map.106 = bf16[512,6144]{1,0:T(8,128)(2,1)} custom-call(bf16[256,1152]{1,0:T(8,128)(2,1)} %get-tuple-element.34.top.refs_0_, bf16[256,1152]{1,0:T(8,128)(2,1)} %get-tuple-element.35.bottom.refs_1_, bf16[6144,1152]{1,0:T(8,128)(2,1)} %all-gather.4.cloned.1.call-done.weight), custom_call_target="tpu_custom_call" | custom-call | flops 7247757312 | bytes 21626880 | tf_op jit(solution)/shard_map/pallas_call | solution.py:357
  174.3 8.2 %collective-permute-done.11.refs_4_ = bf16[256,1152]{1,0:T(8,128)(2,1)S(1)} collective-permute-done((bf16[256,1152]{1,0:T(8,128)(2,1)}, bf16[256,1152]{1,0:T(8,128)(2,1)S(1)}, u32[]{:S(2)}, u32[]{:S(2)}) %collective-permute-start.11) | collective-permute-done | bytes 589856 | tf_op jit(solution)/shard_map/ppermute | solution.py:34
  183.4 3.6 %collective-permute-start.14 = (bf16[256,1152]{1,0:T(8,128)(2,1)}, bf16[256,1152]{1,0:T(8,128)(2,1)S(1)}, u32[]{:S(2)}, u32[]{:S(2)}) collective-permute-start(bf16[256,1152]{1,0:T(8,128)(2,1)} %collective-permute-done.12.refs_5_), channel_id=1, source_target_pairs={{0,24},{8,0},{16,8},{24,16},{32,56},{40,32},{48,40},{56,48},{64,88... | collective-permute-start | bytes 1769480 | tf_op jit(solution)/shard_map/ppermute | solution.py:34
  187.0 2.8 %copy-done = bf16[16,512,384]{2,1,0:T(8,128)(2,1)S(1)} copy-done((bf16[16,512,384]{2,1,0:T(8,128)(2,1)S(1)}, bf16[16,512,384]{2,1,0:T(8,128)(2,1)}, u32[]{:S(2)}) %copy-start) | copy-done | bytes 6291480
  192.0 9.6 %shard_map.107.partial = f32[4,384,1152]{2,1,0:T(8,128)S(1)} custom-call(s32[4]{0:T(128)S(1)} %and_select_fusion.table, bf16[8,2,512,384]{3,2,1,0:T(8,128)(2,1)S(1)} %bitcast.27, bf16[8,2,512,384]{3,2,1,0:T(8,128)(2,1)S(1)} %bitcast.28, bf16[256,1152]{1,0:T(8,128)(2,1)S(1)} %copy-done.2, bf16[256,1152]{1,0:T(8,128)(2,1)S(1)} %copy-done.3, ...), custom_call_target="tpu_custom_call" | custom-call | flops 5435817984 | bytes 11010048 | tf_op jit(solution)/shard_map/pallas_call | solution.py:282
  205.0 2.7 %shard_map.108 = (bf16[3,192,1152]{2,1,0:T(8,128)(2,1)S(1)}, bf16[3,192,1152]{2,1,0:T(8,128)(2,1)S(1)}) custom-call(s32[4]{0:T(128)S(1)} %and_select_fusion.table, f32[4,384,1152]{2,1,0:T(8,128)S(1)} %shard_map.107.partial, bf16[8,2,512,384]{3,2,1,0:T(8,128)(2,1)S(1)} %bitcast.30, bf16[256,1152]{1,0:T(8,128)(2,1)S(1)} %collective-permute-done.13.far_up, ...), custom_call_target="tpu_custom_call" | custom-call | flops 1358954496 | bytes 10321920 | tf_op jit(solution)/shard_map/pallas_call | solution.py:321
  207.8 5.1 %collective-permute-done.15 = bf16[192,1152]{1,0:T(8,128)(2,1)S(1)} collective-permute-done((bf16[192,1152]{1,0:T(8,128)(2,1)S(1)}, bf16[192,1152]{1,0:T(8,128)(2,1)S(1)}, u32[]{:S(2)}, u32[]{:S(2)}) %collective-permute-start.15) | collective-permute-done | bytes 442400 | tf_op jit(solution)/shard_map/ppermute | solution.py:30
  213.1 1.8 collective-permute-start.16
  215.5 16.0 %collective-permute-done.16 = bf16[384,1152]{1,0:T(8,128)(2,1)S(1)} collective-permute-done((bf16[384,1152]{1,0:T(8,128)(2,1)S(1)}, bf16[384,1152]{1,0:T(8,128)(2,1)S(1)}, u32[]{:S(2)}, u32[]{:S(2)}) %collective-permute-start.16) | collective-permute-done | bytes 884768 | tf_op jit(solution)/shard_map/ppermute | solution.py:30
  231.5 3.0 %collective-permute-done.18 = bf16[384,1152]{1,0:T(8,128)(2,1)S(1)} collective-permute-done((bf16[384,1152]{1,0:T(8,128)(2,1)S(1)}, bf16[384,1152]{1,0:T(8,128)(2,1)S(1)}, u32[]{:S(2)}, u32[]{:S(2)}) %collective-permute-start.18) | collective-permute-done | bytes 884768 | tf_op jit(solution)/shard_map/ppermute | solution.py:30
  (98 shorter events, 24.2 us)
Async XLA Ops:
  7.2 124.7 %all-gather.4.cloned.1.call-start = ((), (), s32[]{:S(2)}) async-start(), calls=%async_computation.2 | async-start | bytes 15040512 | tf_op jit(solution)/shard_map/all_gather | solution.py:392
  7.9 179.1 %all-gather.6.cloned.1.call-start = ((), (), s32[]{:S(2)}) async-start(), calls=%async_computation.4 | async-start | bytes 7077888 | tf_op jit(solution)/shard_map/all_gather | solution.py:419
  59.0 28.2 %collective-permute-start = (bf16[512,768]{1,0:T(8,128)(2,1)}, bf16[512,768]{1,0:T(8,128)(2,1)S(1)}, u32[]{:S(2)}, u32[]{:S(2)}) collective-permute-start(bf16[512,768]{1,0:T(8,128)(2,1)} %bitcast.33), channel_id=1, source_target_pairs={{0,2},{1,3},{2,4},{3,5},{4,6},{5,7},{6,0},{7,1},{8,10},{9,11},{10,... | collective-permute-start | bytes 2359304 | tf_op jit(solution)/shard_map/ppermute | solution.py:38
  60.6 26.6 %collective-permute-start.1 = (bf16[512,768]{1,0:T(8,128)(2,1)}, bf16[512,768]{1,0:T(8,128)(2,1)S(1)}, u32[]{:S(2)}, u32[]{:S(2)}) collective-permute-start(bf16[512,768]{1,0:T(8,128)(2,1)} %bitcast.34), channel_id=1, source_target_pairs={{0,6},{1,7},{2,0},{3,1},{4,2},{5,3},{6,4},{7,5},{8,14},{9,15},{10,... | collective-permute-start | bytes 2359304 | tf_op jit(solution)/shard_map/ppermute | solution.py:38
  63.7 23.5 %collective-permute-start.2 = (bf16[512,384]{1,0:T(8,128)(2,1)S(1)}, bf16[512,384]{1,0:T(8,128)(2,1)S(1)}, u32[]{:S(2)}, u32[]{:S(2)}) collective-permute-start(bf16[512,384]{1,0:T(8,128)(2,1)S(1)} %get-tuple-element.55), channel_id=1, source_target_pairs={{0,8},{2,10},{4,12},{6,14},{9,17},{11,19},{13,21},{15,23},{17,25},... | collective-permute-start | bytes 1179656 | tf_op jit(solution)/shard_map/ppermute | solution.py:49
  65.9 21.2 %collective-permute-start.3 = (bf16[512,384]{1,0:T(8,128)(2,1)S(1)}, bf16[512,384]{1,0:T(8,128)(2,1)S(1)}, u32[]{:S(2)}, u32[]{:S(2)}) collective-permute-start(bf16[512,384]{1,0:T(8,128)(2,1)S(1)} %get-tuple-element.55), channel_id=1, source_target_pairs={{1,25},{3,27},{5,29},{7,31},{8,0},{10,2},{12,4},{14,6},{16,8},{18,... | collective-permute-start | bytes 1179656 | tf_op jit(solution)/shard_map/ppermute | solution.py:49
  67.2 20.0 %collective-permute-start.4 = (bf16[512,384]{1,0:T(8,128)(2,1)S(1)}, bf16[512,384]{1,0:T(8,128)(2,1)S(1)}, u32[]{:S(2)}, u32[]{:S(2)}) collective-permute-start(bf16[512,384]{1,0:T(8,128)(2,1)S(1)} %get-tuple-element.28), channel_id=1, source_target_pairs={{1,17},{3,19},{5,21},{7,23},{9,25},{11,27},{13,29},{15,31},{16,0},... | collective-permute-start | bytes 1179656 | tf_op jit(solution)/shard_map/ppermute | solution.py:49
  88.4 14.4 %collective-permute-start.7 = (bf16[2,512,384]{2,1,0:T(8,128)(2,1)}, bf16[2,512,384]{2,1,0:T(8,128)(2,1)}, u32[]{:S(2)}, u32[]{:S(2)}) collective-permute-start(bf16[2,512,384]{2,1,0:T(8,128)(2,1)} %broadcast_select_fusion), channel_id=1, source_target_pairs={{0,1},{1,0},{2,3},{3,2},{4,5},{5,4},{6,7},{7,6},{8,9},{9,8},{10,11... | collective-permute-start | bytes 2359304 | tf_op jit(solution)/shard_map/ppermute | solution.py:53
  88.4 12.9 %collective-permute-start.5 = (bf16[256,768]{1,0:T(8,128)(2,1)S(1)}, bf16[256,768]{1,0:T(8,128)(2,1)}, u32[]{:S(2)}, u32[]{:S(2)}) collective-permute-start(bf16[256,768]{1,0:T(8,128)(2,1)S(1)} %slice.36), channel_id=1, source_target_pairs={{0,2},{1,3},{2,4},{3,5},{4,6},{5,7},{6,0},{7,1},{8,10},{9,11},{10,... | collective-permute-start | bytes 1179656 | tf_op jit(solution)/shard_map/ppermute | solution.py:38
  89.4 12.2 %collective-permute-start.6 = (bf16[256,768]{1,0:T(8,128)(2,1)}, bf16[256,768]{1,0:T(8,128)(2,1)}, u32[]{:S(2)}, u32[]{:S(2)}) collective-permute-start(bf16[256,768]{1,0:T(8,128)(2,1)} %slice.37), channel_id=1, source_target_pairs={{0,6},{1,7},{2,0},{3,1},{4,2},{5,3},{6,4},{7,5},{8,14},{9,15},{10,... | collective-permute-start | bytes 1179656 | tf_op jit(solution)/shard_map/ppermute | solution.py:38
  104.0 131.8 %reduce-scatter.2.cloned.1.call-start = ((), (), s32[]{:S(2)}) async-start(), calls=%async_computation.3 | async-start | bytes 7077888 | tf_op jit(solution)/shard_map/reduce_scatter | solution.py:450
  106.0 6.2 %collective-permute-start.8 = (bf16[4,512,768]{2,1,0:T(8,128)(2,1)}, bf16[4,512,768]{2,1,0:T(8,128)(2,1)}, u32[]{:S(2)}, u32[]{:S(2)}) collective-permute-start(bf16[4,512,768]{2,1,0:T(8,128)(2,1)} %pad_maximum_fusion.own), channel_id=1, source_target_pairs={{0,1},{1,0},{2,3},{3,2},{4,5},{5,4},{6,7},{7,6},{8,9},{9,8},{10,11... | collective-permute-start | bytes 9437192 | tf_op jit(solution)/shard_map/ppermute | solution.py:53
  154.3 20.0 %collective-permute-start.10 = (bf16[256,1152]{1,0:T(8,128)(2,1)}, bf16[256,1152]{1,0:T(8,128)(2,1)S(1)}, u32[]{:S(2)}, u32[]{:S(2)}) collective-permute-start(bf16[256,1152]{1,0:T(8,128)(2,1)} %get-tuple-element.35.bottom.refs_1_), channel_id=1, source_target_pairs={{0,8},{8,16},{16,24},{24,0},{32,40},{40,48},{48,56},{56,32},{64,72... | collective-permute-start | bytes 1769480 | tf_op jit(solution)/shard_map/ppermute | solution.py:34
  154.3 28.2 %collective-permute-start.12 = (bf16[256,1152]{1,0:T(8,128)(2,1)}, bf16[256,1152]{1,0:T(8,128)(2,1)}, u32[]{:S(2)}, u32[]{:S(2)}) collective-permute-start(bf16[256,1152]{1,0:T(8,128)(2,1)} %get-tuple-element.35.bottom.refs_1_), channel_id=1, source_target_pairs={{0,24},{8,0},{16,8},{24,16},{32,56},{40,32},{48,40},{56,48},{64,88... | collective-permute-start | bytes 1769480 | tf_op jit(solution)/shard_map/ppermute | solution.py:34
  157.6 25.0 %collective-permute-start.11 = (bf16[256,1152]{1,0:T(8,128)(2,1)}, bf16[256,1152]{1,0:T(8,128)(2,1)S(1)}, u32[]{:S(2)}, u32[]{:S(2)}) collective-permute-start(bf16[256,1152]{1,0:T(8,128)(2,1)} %get-tuple-element.34.top.refs_0_), channel_id=1, source_target_pairs={{0,24},{8,0},{16,8},{24,16},{32,56},{40,32},{48,40},{56,48},{64,88... | collective-permute-start | bytes 1769480 | tf_op jit(solution)/shard_map/ppermute | solution.py:34
  157.6 25.7 %collective-permute-start.9 = (bf16[256,1152]{1,0:T(8,128)(2,1)}, bf16[256,1152]{1,0:T(8,128)(2,1)}, u32[]{:S(2)}, u32[]{:S(2)}) collective-permute-start(bf16[256,1152]{1,0:T(8,128)(2,1)} %get-tuple-element.34.top.refs_0_), channel_id=1, source_target_pairs={{0,8},{8,16},{16,24},{24,0},{32,40},{40,48},{48,56},{56,32},{64,72... | collective-permute-start | bytes 1769480 | tf_op jit(solution)/shard_map/ppermute | solution.py:34
  174.3 12.7 %copy-start.2 = (bf16[256,1152]{1,0:T(8,128)(2,1)S(1)}, bf16[256,1152]{1,0:T(8,128)(2,1)}, u32[]{:S(2)}) copy-start(bf16[256,1152]{1,0:T(8,128)(2,1)} %get-tuple-element.34.top.refs_0_) | copy-start | bytes 1769476
  174.3 12.7 %copy-start.3 = (bf16[256,1152]{1,0:T(8,128)(2,1)S(1)}, bf16[256,1152]{1,0:T(8,128)(2,1)}, u32[]{:S(2)}) copy-start(bf16[256,1152]{1,0:T(8,128)(2,1)} %get-tuple-element.35.bottom.refs_1_) | copy-start | bytes 1769476
  183.4 18.2 %collective-permute-start.13 = (bf16[256,1152]{1,0:T(8,128)(2,1)}, bf16[256,1152]{1,0:T(8,128)(2,1)S(1)}, u32[]{:S(2)}, u32[]{:S(2)}) collective-permute-start(bf16[256,1152]{1,0:T(8,128)(2,1)} %collective-permute-done.9.refs_2_), channel_id=1, source_target_pairs={{0,8},{8,16},{16,24},{24,0},{32,40},{40,48},{48,56},{56,32},{64,72... | collective-permute-start | bytes 1769480 | tf_op jit(solution)/shard_map/ppermute | solution.py:34
  183.4 18.2 %collective-permute-start.14 = (bf16[256,1152]{1,0:T(8,128)(2,1)}, bf16[256,1152]{1,0:T(8,128)(2,1)S(1)}, u32[]{:S(2)}, u32[]{:S(2)}) collective-permute-start(bf16[256,1152]{1,0:T(8,128)(2,1)} %collective-permute-done.12.refs_5_), channel_id=1, source_target_pairs={{0,24},{8,0},{16,8},{24,16},{32,56},{40,32},{48,40},{56,48},{64,88... | collective-permute-start | bytes 1769480 | tf_op jit(solution)/shard_map/ppermute | solution.py:34
  202.9 10.0 %collective-permute-start.15 = (bf16[192,1152]{1,0:T(8,128)(2,1)S(1)}, bf16[192,1152]{1,0:T(8,128)(2,1)S(1)}, u32[]{:S(2)}, u32[]{:S(2)}) collective-permute-start(bf16[192,1152]{1,0:T(8,128)(2,1)S(1)} %bitcast.32), channel_id=1, source_target_pairs={{0,32},{8,40},{16,48},{24,56},{32,64},{40,72},{48,80},{56,88},{64,... | collective-permute-start | bytes 1327112 | tf_op jit(solution)/shard_map/ppermute | solution.py:30
  203.7 11.2 %collective-permute-start.17 = (bf16[192,1152]{1,0:T(8,128)(2,1)S(1)}, bf16[192,1152]{1,0:T(8,128)(2,1)S(1)}, u32[]{:S(2)}, u32[]{:S(2)}) collective-permute-start(bf16[192,1152]{1,0:T(8,128)(2,1)S(1)} %bitcast.31), channel_id=1, source_target_pairs={{0,96},{8,104},{16,112},{24,120},{32,0},{40,8},{48,16},{56,24},{64... | collective-permute-start | bytes 1327112 | tf_op jit(solution)/shard_map/ppermute | solution.py:30
  213.1 18.4 %collective-permute-start.16 = (bf16[384,1152]{1,0:T(8,128)(2,1)S(1)}, bf16[384,1152]{1,0:T(8,128)(2,1)S(1)}, u32[]{:S(2)}, u32[]{:S(2)}) collective-permute-start(bf16[384,1152]{1,0:T(8,128)(2,1)S(1)} %pad_maximum_fusion.1), channel_id=1, source_target_pairs={{0,32},{8,40},{16,48},{24,56},{32,64},{40,72},{48,80},{56,88},{64,... | collective-permute-start | bytes 2654216 | tf_op jit(solution)/shard_map/ppermute | solution.py:30
  215.1 19.4 %collective-permute-start.18 = (bf16[384,1152]{1,0:T(8,128)(2,1)S(1)}, bf16[384,1152]{1,0:T(8,128)(2,1)S(1)}, u32[]{:S(2)}, u32[]{:S(2)}) collective-permute-start(bf16[384,1152]{1,0:T(8,128)(2,1)S(1)} %pad_maximum_fusion.2), channel_id=1, source_target_pairs={{0,96},{8,104},{16,112},{24,120},{32,0},{40,8},{48,16},{56,24},{64... | collective-permute-start | bytes 2654216 | tf_op jit(solution)/shard_map/ppermute | solution.py:30
  (19 other events, 91.6 us)
Sparse Core Ops, SparseCore 0:
  10.2 121.6 all-gather.3
  134.1 39.8 all-gather.5
  183.4 43.5 reduce-scatter.1

commit v2 on v1

--- a/solution.py
+++ b/solution.py
@@ -169,15 +169,15 @@
     weights = jnp.where(seg_col == seg_row, weights, 0.0)
     probs = weights * (1.0 / jnp.sum(weights, axis=-1, keepdims=True))
     probs_half = probs.astype(jnp.bfloat16)
-    out = dot(probs_half, value, 1, 0).astype(jnp.bfloat16)
+    out = dot(probs_half, value, 1, 0)
     grad_value = dot(probs_half, up, 0, 0)
     grad_probs = dot(up, value, 1, 1)
-    inner = jnp.sum(probs * grad_probs, axis=-1, keepdims=True)
+    inner = jnp.sum(up.astype(jnp.float32) * out, axis=-1, keepdims=True)
     grad_scores = (probs * (grad_probs - inner) * factor).astype(jnp.bfloat16)
     grad_query = norm_grad(dot(grad_scores, key, 1, 0), query_hat, query_inv, gain_query)
     grad_key = norm_grad(dot(grad_scores, query, 0, 0), key_hat, key_inv, gain_key)
     grads = (grad_query, grad_key, grad_value)
-    return out, [part.astype(jnp.bfloat16) for part in grads]
+    return out.astype(jnp.bfloat16), [part.astype(jnp.bfloat16) for part in grads]
 
 
 def heads_kernel(

time: 243 us -> 243 us (level)
  no operation moved by 1% of the time
where the time goes in v2:
time: 243 us; the launch traced here: 242 us
  waiting for transfers between devices  84.3 us (35%)
  Pallas kernels  55.8 us (23%)
  blocking collectives  44.3 us (18%)
  starting transfers between devices  25.3 us (10%)
  between operations  14.1 us (6%)
  other arithmetic  9.99 us (4%)
  local copies, waits for them, and re-layouts  8.23 us (3%)
    all_to_all x1, blocking collectives, shards(): lax.all_to_all(outgoing, 'row', split_axis=0, concat_axis=0, tiled=True)  44.3 us
    ppermute x4, waiting for transfers between devices, send_x(): return lax.ppermute(values, 'row', along_row(step, 0))  24.2 us
    pallas_call x1, Pallas kernels, run_heads(): pl.pallas_call(heads_kernel, out_shape=(jax.ShapeDtypeStruct((rows, heads...  22.2 us
    all_gather x1, waiting for transfers between devices, shards(): weight_panel = lax.all_gather(qkv_weight, 'row', axis=0, tiled=True)  19.6 us
    ppermute x3, waiting for transfers between devices, send_to_half(): return lax.ppermute(values, ('row', 'col'), pairs)  18.6 us
    pallas_call x1, Pallas kernels, row_terms(): pl.pallas_call(terms_kernel, out_shape=jax.ShapeDtypeStruct((rows, depth)...  14.5 us
    pallas_call x1, Pallas kernels, weigh_near(): pl.pallas_call(weigh_near_kernel, out_shape=jax.ShapeDtypeStruct((pieces,...  9.63 us
    ppermute x6, waiting for transfers between devices, send_z(): return lax.ppermute(values, 'row', along_row(0, step))  9.16 us
  transfers between devices with their start and end apart: 22, of which 10 were waited for; matrix products, arithmetic and copies ran while one was open for 5% of the time, Pallas kernels for 23%

profile of v2, /device:TPU:6, one launch (start us, length us, event | category | flops | bytes accessed | tf_op | source)
XLA Modules:
  0.0 242.0 jit_solution(7581034472328885313)
XLA Ops:
  7.9 2.9 %shard_map.103 = bf16[16,32,1664]{2,1,0:T(8,128)(2,1)} custom-call(s32[16]{0:T(128)} %packing.1, bf16[16,32,768]{2,1,0:T(8,128)(2,1)} %blocks.1), custom_call_target="tpu_custom_call" | custom-call | tf_op jit(solution)/shard_map/pallas_call | solution.py:92
  10.9 44.3 %all_to_all.5.arrived = bf16[16,32,1664]{2,1,0:T(8,128)(2,1)S(1)} all-to-all(bf16[16,32,1664]{2,1,0:T(8,128)(2,1)} %shard_map.103), channel_id=1, replica_groups=mesh['row'=16,'col'=8] {'row'}, dimensions={0} | all-to-all | bytes 3407872 | tf_op jit(solution)/shard_map/all_to_all | solution.py:398
  56.4 2.6 %shard_map.104 = bf16[16,32,768]{2,1,0:T(8,128)(2,1)} custom-call(s32[16]{0:T(128)} %select_reduce_fusion.where, bf16[16,32,1664]{2,1,0:T(8,128)(2,1)} %copy-done.9), custom_call_target="tpu_custom_call" | custom-call | tf_op jit(solution)/shard_map/pallas_call | solution.py:129
  60.6 1.7 collective-permute-start.1
  63.7 2.2 collective-permute-start.2
  68.5 18.6 %collective-permute-done.2 = bf16[512,384]{1,0:T(8,128)(2,1)S(1)} collective-permute-done((bf16[512,384]{1,0:T(8,128)(2,1)S(1)}, bf16[512,384]{1,0:T(8,128)(2,1)S(1)}, u32[]{:S(2)}, u32[]{:S(2)}) %collective-permute-start.2) | collective-permute-done | bytes 393248 | tf_op jit(solution)/shard_map/ppermute | solution.py:49
  89.4 3.2 %collective-permute-start.6 = (bf16[256,768]{1,0:T(8,128)(2,1)}, bf16[256,768]{1,0:T(8,128)(2,1)}, u32[]{:S(2)}, u32[]{:S(2)}) collective-permute-start(bf16[256,768]{1,0:T(8,128)(2,1)} %slice.37), channel_id=1, source_target_pairs={{0,6},{1,7},{2,0},{3,1},{4,2},{5,3},{6,4},{7,5},{8,14},{9,15},{10,... | collective-permute-start | bytes 1179656 | tf_op jit(solution)/shard_map/ppermute | solution.py:38
  92.6 8.8 %collective-permute-done.5 = bf16[256,768]{1,0:T(8,128)(2,1)} collective-permute-done((bf16[256,768]{1,0:T(8,128)(2,1)S(1)}, bf16[256,768]{1,0:T(8,128)(2,1)}, u32[]{:S(2)}, u32[]{:S(2)}) %collective-permute-start.5) | collective-permute-done | bytes 393248 | tf_op jit(solution)/shard_map/ppermute | solution.py:38
  104.1 1.9 pad_maximum_fusion.own
  109.3 2.9 %collective-permute-done.8.other = bf16[4,512,768]{2,1,0:T(8,128)(2,1)} collective-permute-done((bf16[4,512,768]{2,1,0:T(8,128)(2,1)}, bf16[4,512,768]{2,1,0:T(8,128)(2,1)}, u32[]{:S(2)}, u32[]{:S(2)}) %collective-permute-start.8) | collective-permute-done | bytes 3145760 | tf_op jit(solution)/shard_map/ppermute | solution.py:53
  112.2 19.6 %all-gather.4.cloned.1.call-done.weight = bf16[6144,1152]{1,0:T(8,128)(2,1)} async-done(((bf16[384,1152]{1,0:T(8,128)(2,1)}), bf16[6144,1152]{1,0:T(8,128)(2,1)}) %all-gather.4.cloned.1.call-update) | async-done | bytes 14155792 | tf_op jit(solution)/shard_map/all_gather | solution.py:392
  131.9 22.2 %shard_map.105 = (bf16[512,384]{1,0:T(8,128)(2,1)}, bf16[256,1152]{1,0:T(8,128)(2,1)}, bf16[256,1152]{1,0:T(8,128)(2,1)}) custom-call(s32[8]{0:T(128)} %pad_add_fusion.order, bf16[4,512,768]{2,1,0:T(8,128)(2,1)} %pad_maximum_fusion.own, bf16[4,512,768]{2,1,0:T(8,128)(2,1)} %collective-permute-done.8.other, ...), custom_call_target="tpu_custom_call" | custom-call | flops 7247757312 | bytes 20447232 | tf_op jit(solution)/shard_map/pallas_call | solution.py:226
  154.1 3.2 %collective-permute-start.12 = (bf16[256,1152]{1,0:T(8,128)(2,1)}, bf16[256,1152]{1,0:T(8,128)(2,1)}, u32[]{:S(2)}, u32[]{:S(2)}) collective-permute-start(bf16[256,1152]{1,0:T(8,128)(2,1)} %get-tuple-element.35.bottom.refs_1_), channel_id=1, source_target_pairs={{0,24},{8,0},{16,8},{24,16},{32,56},{40,32},{48,40},{56,48},{64,88... | collective-permute-start | bytes 1769480 | tf_op jit(solution)/shard_map/ppermute | solution.py:34
  157.3 2.0 collective-permute-start.9
  159.3 14.5 %shard_map.106 = bf16[512,6144]{1,0:T(8,128)(2,1)} custom-call(bf16[256,1152]{1,0:T(8,128)(2,1)} %get-tuple-element.34.top.refs_0_, bf16[256,1152]{1,0:T(8,128)(2,1)} %get-tuple-element.35.bottom.refs_1_, bf16[6144,1152]{1,0:T(8,128)(2,1)} %all-gather.4.cloned.1.call-done.weight), custom_call_target="tpu_custom_call" | custom-call | flops 7247757312 | bytes 21626880 | tf_op jit(solution)/shard_map/pallas_call | solution.py:357
  173.8 8.4 %collective-permute-done.11.refs_4_ = bf16[256,1152]{1,0:T(8,128)(2,1)S(1)} collective-permute-done((bf16[256,1152]{1,0:T(8,128)(2,1)}, bf16[256,1152]{1,0:T(8,128)(2,1)S(1)}, u32[]{:S(2)}, u32[]{:S(2)}) %collective-permute-start.11) | collective-permute-done | bytes 589856 | tf_op jit(solution)/shard_map/ppermute | solution.py:34
  183.1 3.6 %collective-permute-start.14 = (bf16[256,1152]{1,0:T(8,128)(2,1)}, bf16[256,1152]{1,0:T(8,128)(2,1)S(1)}, u32[]{:S(2)}, u32[]{:S(2)}) collective-permute-start(bf16[256,1152]{1,0:T(8,128)(2,1)} %collective-permute-done.12.refs_5_), channel_id=1, source_target_pairs={{0,24},{8,0},{16,8},{24,16},{32,56},{40,32},{48,40},{56,48},{64,88... | collective-permute-start | bytes 1769480 | tf_op jit(solution)/shard_map/ppermute | solution.py:34
  186.8 2.8 %copy-done = bf16[16,512,384]{2,1,0:T(8,128)(2,1)S(1)} copy-done((bf16[16,512,384]{2,1,0:T(8,128)(2,1)S(1)}, bf16[16,512,384]{2,1,0:T(8,128)(2,1)}, u32[]{:S(2)}) %copy-start) | copy-done | bytes 6291480
  191.7 9.6 %shard_map.107.partial = f32[4,384,1152]{2,1,0:T(8,128)S(1)} custom-call(s32[4]{0:T(128)S(1)} %and_select_fusion.table, bf16[8,2,512,384]{3,2,1,0:T(8,128)(2,1)S(1)} %bitcast.27, bf16[8,2,512,384]{3,2,1,0:T(8,128)(2,1)S(1)} %bitcast.28, bf16[256,1152]{1,0:T(8,128)(2,1)S(1)} %copy-done.2, bf16[256,1152]{1,0:T(8,128)(2,1)S(1)} %copy-done.3, ...), custom_call_target="tpu_custom_call" | custom-call | flops 5435817984 | bytes 11010048 | tf_op jit(solution)/shard_map/pallas_call | solution.py:282
  204.7 2.7 %shard_map.108 = (bf16[3,192,1152]{2,1,0:T(8,128)(2,1)S(1)}, bf16[3,192,1152]{2,1,0:T(8,128)(2,1)S(1)}) custom-call(s32[4]{0:T(128)S(1)} %and_select_fusion.table, f32[4,384,1152]{2,1,0:T(8,128)S(1)} %shard_map.107.partial, bf16[8,2,512,384]{3,2,1,0:T(8,128)(2,1)S(1)} %bitcast.30, bf16[256,1152]{1,0:T(8,128)(2,1)S(1)} %collective-permute-done.13.far_up, ...), custom_call_target="tpu_custom_call" | custom-call | flops 1358954496 | bytes 10321920 | tf_op jit(solution)/shard_map/pallas_call | solution.py:321
  207.5 5.1 %collective-permute-done.15 = bf16[192,1152]{1,0:T(8,128)(2,1)S(1)} collective-permute-done((bf16[192,1152]{1,0:T(8,128)(2,1)S(1)}, bf16[192,1152]{1,0:T(8,128)(2,1)S(1)}, u32[]{:S(2)}, u32[]{:S(2)}) %collective-permute-start.15) | collective-permute-done | bytes 442400 | tf_op jit(solution)/shard_map/ppermute | solution.py:30
  212.8 1.8 collective-permute-start.16
  215.2 16.0 %collective-permute-done.16 = bf16[384,1152]{1,0:T(8,128)(2,1)S(1)} collective-permute-done((bf16[384,1152]{1,0:T(8,128)(2,1)S(1)}, bf16[384,1152]{1,0:T(8,128)(2,1)S(1)}, u32[]{:S(2)}, u32[]{:S(2)}) %collective-permute-start.16) | collective-permute-done | bytes 884768 | tf_op jit(solution)/shard_map/ppermute | solution.py:30
  231.2 3.1 %collective-permute-done.18 = bf16[384,1152]{1,0:T(8,128)(2,1)S(1)} collective-permute-done((bf16[384,1152]{1,0:T(8,128)(2,1)S(1)}, bf16[384,1152]{1,0:T(8,128)(2,1)S(1)}, u32[]{:S(2)}, u32[]{:S(2)}) %collective-permute-start.18) | collective-permute-done | bytes 884768 | tf_op jit(solution)/shard_map/ppermute | solution.py:30
  (98 shorter events, 24.2 us)
Async XLA Ops:
  7.2 124.7 %all-gather.4.cloned.1.call-start = ((), (), s32[]{:S(2)}) async-start(), calls=%async_computation.2 | async-start | bytes 15040512 | tf_op jit(solution)/shard_map/all_gather | solution.py:392
  7.9 178.8 %all-gather.6.cloned.1.call-start = ((), (), s32[]{:S(2)}) async-start(), calls=%async_computation.4 | async-start | bytes 7077888 | tf_op jit(solution)/shard_map/all_gather | solution.py:419
  59.0 28.2 %collective-permute-start = (bf16[512,768]{1,0:T(8,128)(2,1)}, bf16[512,768]{1,0:T(8,128)(2,1)S(1)}, u32[]{:S(2)}, u32[]{:S(2)}) collective-permute-start(bf16[512,768]{1,0:T(8,128)(2,1)} %bitcast.33), channel_id=1, source_target_pairs={{0,2},{1,3},{2,4},{3,5},{4,6},{5,7},{6,0},{7,1},{8,10},{9,11},{10,... | collective-permute-start | bytes 2359304 | tf_op jit(solution)/shard_map/ppermute | solution.py:38
  60.6 26.6 %collective-permute-start.1 = (bf16[512,768]{1,0:T(8,128)(2,1)}, bf16[512,768]{1,0:T(8,128)(2,1)S(1)}, u32[]{:S(2)}, u32[]{:S(2)}) collective-permute-start(bf16[512,768]{1,0:T(8,128)(2,1)} %bitcast.34), channel_id=1, source_target_pairs={{0,6},{1,7},{2,0},{3,1},{4,2},{5,3},{6,4},{7,5},{8,14},{9,15},{10,... | collective-permute-start | bytes 2359304 | tf_op jit(solution)/shard_map/ppermute | solution.py:38
  63.7 23.5 %collective-permute-start.2 = (bf16[512,384]{1,0:T(8,128)(2,1)S(1)}, bf16[512,384]{1,0:T(8,128)(2,1)S(1)}, u32[]{:S(2)}, u32[]{:S(2)}) collective-permute-start(bf16[512,384]{1,0:T(8,128)(2,1)S(1)} %get-tuple-element.55), channel_id=1, source_target_pairs={{0,8},{2,10},{4,12},{6,14},{9,17},{11,19},{13,21},{15,23},{17,25},... | collective-permute-start | bytes 1179656 | tf_op jit(solution)/shard_map/ppermute | solution.py:49
  65.9 21.2 %collective-permute-start.3 = (bf16[512,384]{1,0:T(8,128)(2,1)S(1)}, bf16[512,384]{1,0:T(8,128)(2,1)S(1)}, u32[]{:S(2)}, u32[]{:S(2)}) collective-permute-start(bf16[512,384]{1,0:T(8,128)(2,1)S(1)} %get-tuple-element.55), channel_id=1, source_target_pairs={{1,25},{3,27},{5,29},{7,31},{8,0},{10,2},{12,4},{14,6},{16,8},{18,... | collective-permute-start | bytes 1179656 | tf_op jit(solution)/shard_map/ppermute | solution.py:49
  67.2 20.0 %collective-permute-start.4 = (bf16[512,384]{1,0:T(8,128)(2,1)S(1)}, bf16[512,384]{1,0:T(8,128)(2,1)S(1)}, u32[]{:S(2)}, u32[]{:S(2)}) collective-permute-start(bf16[512,384]{1,0:T(8,128)(2,1)S(1)} %get-tuple-element.28), channel_id=1, source_target_pairs={{1,17},{3,19},{5,21},{7,23},{9,25},{11,27},{13,29},{15,31},{16,0},... | collective-permute-start | bytes 1179656 | tf_op jit(solution)/shard_map/ppermute | solution.py:49
  88.4 14.4 %collective-permute-start.7 = (bf16[2,512,384]{2,1,0:T(8,128)(2,1)}, bf16[2,512,384]{2,1,0:T(8,128)(2,1)}, u32[]{:S(2)}, u32[]{:S(2)}) collective-permute-start(bf16[2,512,384]{2,1,0:T(8,128)(2,1)} %broadcast_select_fusion), channel_id=1, source_target_pairs={{0,1},{1,0},{2,3},{3,2},{4,5},{5,4},{6,7},{7,6},{8,9},{9,8},{10,11... | collective-permute-start | bytes 2359304 | tf_op jit(solution)/shard_map/ppermute | solution.py:53
  88.4 12.9 %collective-permute-start.5 = (bf16[256,768]{1,0:T(8,128)(2,1)S(1)}, bf16[256,768]{1,0:T(8,128)(2,1)}, u32[]{:S(2)}, u32[]{:S(2)}) collective-permute-start(bf16[256,768]{1,0:T(8,128)(2,1)S(1)} %slice.36), channel_id=1, source_target_pairs={{0,2},{1,3},{2,4},{3,5},{4,6},{5,7},{6,0},{7,1},{8,10},{9,11},{10,... | collective-permute-start | bytes 1179656 | tf_op jit(solution)/shard_map/ppermute | solution.py:38
  89.4 12.2 %collective-permute-start.6 = (bf16[256,768]{1,0:T(8,128)(2,1)}, bf16[256,768]{1,0:T(8,128)(2,1)}, u32[]{:S(2)}, u32[]{:S(2)}) collective-permute-start(bf16[256,768]{1,0:T(8,128)(2,1)} %slice.37), channel_id=1, source_target_pairs={{0,6},{1,7},{2,0},{3,1},{4,2},{5,3},{6,4},{7,5},{8,14},{9,15},{10,... | collective-permute-start | bytes 1179656 | tf_op jit(solution)/shard_map/ppermute | solution.py:38
  104.0 131.5 %reduce-scatter.2.cloned.1.call-start = ((), (), s32[]{:S(2)}) async-start(), calls=%async_computation.3 | async-start | bytes 7077888 | tf_op jit(solution)/shard_map/reduce_scatter | solution.py:450
  106.0 6.2 %collective-permute-start.8 = (bf16[4,512,768]{2,1,0:T(8,128)(2,1)}, bf16[4,512,768]{2,1,0:T(8,128)(2,1)}, u32[]{:S(2)}, u32[]{:S(2)}) collective-permute-start(bf16[4,512,768]{2,1,0:T(8,128)(2,1)} %pad_maximum_fusion.own), channel_id=1, source_target_pairs={{0,1},{1,0},{2,3},{3,2},{4,5},{5,4},{6,7},{7,6},{8,9},{9,8},{10,11... | collective-permute-start | bytes 9437192 | tf_op jit(solution)/shard_map/ppermute | solution.py:53
  154.1 19.8 %collective-permute-start.10 = (bf16[256,1152]{1,0:T(8,128)(2,1)}, bf16[256,1152]{1,0:T(8,128)(2,1)S(1)}, u32[]{:S(2)}, u32[]{:S(2)}) collective-permute-start(bf16[256,1152]{1,0:T(8,128)(2,1)} %get-tuple-element.35.bottom.refs_1_), channel_id=1, source_target_pairs={{0,8},{8,16},{16,24},{24,0},{32,40},{40,48},{48,56},{56,32},{64,72... | collective-permute-start | bytes 1769480 | tf_op jit(solution)/shard_map/ppermute | solution.py:34
  154.1 28.2 %collective-permute-start.12 = (bf16[256,1152]{1,0:T(8,128)(2,1)}, bf16[256,1152]{1,0:T(8,128)(2,1)}, u32[]{:S(2)}, u32[]{:S(2)}) collective-permute-start(bf16[256,1152]{1,0:T(8,128)(2,1)} %get-tuple-element.35.bottom.refs_1_), channel_id=1, source_target_pairs={{0,24},{8,0},{16,8},{24,16},{32,56},{40,32},{48,40},{56,48},{64,88... | collective-permute-start | bytes 1769480 | tf_op jit(solution)/shard_map/ppermute | solution.py:34
  157.3 25.0 %collective-permute-start.11 = (bf16[256,1152]{1,0:T(8,128)(2,1)}, bf16[256,1152]{1,0:T(8,128)(2,1)S(1)}, u32[]{:S(2)}, u32[]{:S(2)}) collective-permute-start(bf16[256,1152]{1,0:T(8,128)(2,1)} %get-tuple-element.34.top.refs_0_), channel_id=1, source_target_pairs={{0,24},{8,0},{16,8},{24,16},{32,56},{40,32},{48,40},{56,48},{64,88... | collective-permute-start | bytes 1769480 | tf_op jit(solution)/shard_map/ppermute | solution.py:34
  157.3 25.7 %collective-permute-start.9 = (bf16[256,1152]{1,0:T(8,128)(2,1)}, bf16[256,1152]{1,0:T(8,128)(2,1)}, u32[]{:S(2)}, u32[]{:S(2)}) collective-permute-start(bf16[256,1152]{1,0:T(8,128)(2,1)} %get-tuple-element.34.top.refs_0_), channel_id=1, source_target_pairs={{0,8},{8,16},{16,24},{24,0},{32,40},{40,48},{48,56},{56,32},{64,72... | collective-permute-start | bytes 1769480 | tf_op jit(solution)/shard_map/ppermute | solution.py:34
  173.8 12.9 %copy-start.2 = (bf16[256,1152]{1,0:T(8,128)(2,1)S(1)}, bf16[256,1152]{1,0:T(8,128)(2,1)}, u32[]{:S(2)}) copy-start(bf16[256,1152]{1,0:T(8,128)(2,1)} %get-tuple-element.34.top.refs_0_) | copy-start | bytes 1769476
  173.8 12.9 %copy-start.3 = (bf16[256,1152]{1,0:T(8,128)(2,1)S(1)}, bf16[256,1152]{1,0:T(8,128)(2,1)}, u32[]{:S(2)}) copy-start(bf16[256,1152]{1,0:T(8,128)(2,1)} %get-tuple-element.35.bottom.refs_1_) | copy-start | bytes 1769476
  183.1 18.2 %collective-permute-start.13 = (bf16[256,1152]{1,0:T(8,128)(2,1)}, bf16[256,1152]{1,0:T(8,128)(2,1)S(1)}, u32[]{:S(2)}, u32[]{:S(2)}) collective-permute-start(bf16[256,1152]{1,0:T(8,128)(2,1)} %collective-permute-done.9.refs_2_), channel_id=1, source_target_pairs={{0,8},{8,16},{16,24},{24,0},{32,40},{40,48},{48,56},{56,32},{64,72... | collective-permute-start | bytes 1769480 | tf_op jit(solution)/shard_map/ppermute | solution.py:34
  183.1 18.2 %collective-permute-start.14 = (bf16[256,1152]{1,0:T(8,128)(2,1)}, bf16[256,1152]{1,0:T(8,128)(2,1)S(1)}, u32[]{:S(2)}, u32[]{:S(2)}) collective-permute-start(bf16[256,1152]{1,0:T(8,128)(2,1)} %collective-permute-done.12.refs_5_), channel_id=1, source_target_pairs={{0,24},{8,0},{16,8},{24,16},{32,56},{40,32},{48,40},{56,48},{64,88... | collective-permute-start | bytes 1769480 | tf_op jit(solution)/shard_map/ppermute | solution.py:34
  202.6 10.0 %collective-permute-start.15 = (bf16[192,1152]{1,0:T(8,128)(2,1)S(1)}, bf16[192,1152]{1,0:T(8,128)(2,1)S(1)}, u32[]{:S(2)}, u32[]{:S(2)}) collective-permute-start(bf16[192,1152]{1,0:T(8,128)(2,1)S(1)} %bitcast.32), channel_id=1, source_target_pairs={{0,32},{8,40},{16,48},{24,56},{32,64},{40,72},{48,80},{56,88},{64,... | collective-permute-start | bytes 1327112 | tf_op jit(solution)/shard_map/ppermute | solution.py:30
  203.4 11.2 %collective-permute-start.17 = (bf16[192,1152]{1,0:T(8,128)(2,1)S(1)}, bf16[192,1152]{1,0:T(8,128)(2,1)S(1)}, u32[]{:S(2)}, u32[]{:S(2)}) collective-permute-start(bf16[192,1152]{1,0:T(8,128)(2,1)S(1)} %bitcast.31), channel_id=1, source_target_pairs={{0,96},{8,104},{16,112},{24,120},{32,0},{40,8},{48,16},{56,24},{64... | collective-permute-start | bytes 1327112 | tf_op jit(solution)/shard_map/ppermute | solution.py:30
  212.8 18.4 %collective-permute-start.16 = (bf16[384,1152]{1,0:T(8,128)(2,1)S(1)}, bf16[384,1152]{1,0:T(8,128)(2,1)S(1)}, u32[]{:S(2)}, u32[]{:S(2)}) collective-permute-start(bf16[384,1152]{1,0:T(8,128)(2,1)S(1)} %pad_maximum_fusion.1), channel_id=1, source_target_pairs={{0,32},{8,40},{16,48},{24,56},{32,64},{40,72},{48,80},{56,88},{64,... | collective-permute-start | bytes 2654216 | tf_op jit(solution)/shard_map/ppermute | solution.py:30
  214.8 19.4 %collective-permute-start.18 = (bf16[384,1152]{1,0:T(8,128)(2,1)S(1)}, bf16[384,1152]{1,0:T(8,128)(2,1)S(1)}, u32[]{:S(2)}, u32[]{:S(2)}) collective-permute-start(bf16[384,1152]{1,0:T(8,128)(2,1)S(1)} %pad_maximum_fusion.2), channel_id=1, source_target_pairs={{0,96},{8,104},{16,112},{24,120},{32,0},{40,8},{48,16},{56,24},{64... | collective-permute-start | bytes 2654216 | tf_op jit(solution)/shard_map/ppermute | solution.py:30
  (19 other events, 92.0 us)
Sparse Core Ops, SparseCore 0:
  10.2 121.6 all-gather.3
  134.1 39.8 all-gather.5
  183.1 43.5 reduce-scatter.1
